TPU v7x, 128 devices: a whole 4x4x4 slice. The times are simulated.
128 devices in a mesh: row: 8 (over y, x_lo), col: 8 (over z, x_hi), panel: 2 (over core).
Axes of the slice: x: 4 (x_hi: 2, x_lo: 2; x = x_hi * 2 + x_lo), y: 4, z: 4, core: 2. Of those that a mesh axis runs over, the one named last changes fastest.
Arguments:
- basis_values: bfloat16 [2048, 2048, 128], P(('row', 'col', 'panel')), may hold values from -6 to 6
- potential: float32 [262144], P(('row', 'col', 'panel')), may hold values from -0.0009765625 to 0.0009765625
- pair_atoms: int32 [2, 16384], P(None, ('row', 'col', 'panel')), may hold values from 0 to 15
- target_device: int32 [16384, 1], P(('row', 'col', 'panel')), may hold values from 0 to 127; in each aligned block of 128 rows (0 to 127, 128 to 255, ...) at most 2 rows name the same one
- target_block: int32 [16384], P(('row', 'col', 'panel')), may hold values from 0 to 1
- density: bfloat16 [2048, 2048], P('row', 'col'), may hold values from -0.21875 to 0.21875
- density_mask: int32 [16, 16], P('row', 'col'), may hold values 0 or 1
- inverse_intersection: bfloat16 [2048, 4096], P('row', 'col'), may hold values from -6 to 6
- inverse_mask: int32 [16, 32], P('row', 'col'), may hold values 0 or 1
Outputs:
- gradient: float32 [2048, 4096], P('row', ('col', 'panel'))
Inputs may be any that keep to these rules, and one draw needn't show every extreme that they name: `target_device`: among the 128 rows of one device no owner appears more than 2 times.
All inputs are finite; a program needn't handle non-finite values. No bound on the sum of `density_mask` or of `inverse_mask` on one device may be relied on, other than what follows from the above.
Results may differ from a plain program's by a relative error of at most 0.0058.
Values may be sent and summed in bfloat16 or wider, within the bound.
A program may use at most 128 MiB of HBM per device.

v0:
```python
import math

import jax
import jax.numpy as jnp
from jax import lax
from jax.sharding import PartitionSpec as P


def shifted_2(block, axis, distance):
    devices = range(lax.axis_size(axis))
    route = [((i - distance) % len(devices), i) for i in devices]
    return lax.ppermute(block, axis, route)


def from_everyone(value, axis):
    count = lax.axis_size(axis)
    return lax.all_to_all(
        jnp.broadcast_to(value[None], (count, *value.shape)), axis, 0, 0, tiled=True
    )


def of_everyone(value, axis):
    return from_everyone(value, axis).sum(axis=0)


def cut_along(value, dim, count):
    before, after = (value.shape[:dim], value.shape[dim + 1 :])
    return jnp.moveaxis(value.reshape(*before, count, -1, *after), dim, 0)


def sent_and_summed(value, axis, dim):
    tiles = cut_along(value, dim, lax.axis_size(axis))
    arrived = lax.all_to_all(tiles, axis, split_axis=0, concat_axis=0, tiled=True)
    return arrived.sum(axis=0)


def masked_blocks(matrix, block_mask, block_size):
    mask_rows, mask_cols = block_mask.shape
    shaped = matrix.reshape(mask_rows, block_size, mask_cols, block_size)
    factor = block_mask.astype(matrix.dtype)[:, None, :, None]
    return (shaped * factor).reshape(mask_rows * block_size, mask_cols * block_size)


def rotate_cols(tile_value, amount, loop_size):
    for bit_number in range((loop_size - 1).bit_length()):
        shifted = shifted_2(tile_value, "col", -(1 << bit_number))
        tile_value = jnp.where((amount >> bit_number) % 2 == 1, shifted, tile_value)
    return tile_value


def rotate_rows(tile_value, amount, loop_size):
    for bit_number in range((loop_size - 1).bit_length()):
        shifted = shifted_2(tile_value, "row", -(1 << bit_number))
        tile_value = jnp.where((amount >> bit_number) % 2 == 1, shifted, tile_value)
    return tile_value


def cannon_product(left_tile, right_tile, offset, step_count):
    loop_size = lax.axis_size("col")
    left_tile = rotate_cols(left_tile, (lax.axis_index("row") + offset) % loop_size, loop_size)
    right_tile = rotate_rows(right_tile, (lax.axis_index("col") + offset) % loop_size, loop_size)
    accumulated = jnp.dot(left_tile, right_tile, preferred_element_type=jnp.float32)

    def advance(turn_index, state_tuple):
        running, left_now, right_now = state_tuple
        left_now = shifted_2(left_now, "col", -1)
        right_now = shifted_2(right_now, "row", -1)
        running = running + jnp.dot(left_now, right_now, preferred_element_type=jnp.float32)
        return (running, left_now, right_now)

    accumulated, left_tile, right_tile = lax.fori_loop(
        0, step_count - 1, advance, (accumulated, left_tile, right_tile)
    )
    return accumulated


def local(
    basis_values,
    potential,
    pair_atoms,
    target_device,
    target_block,
    density,
    density_mask,
    inverse_intersection,
    inverse_mask,
):
    block_size = basis_values.shape[2]
    part_count = pair_atoms.shape[1]
    layers = lax.axis_size("panel")
    devices = lax.axis_size("row") * lax.axis_size("col") * layers
    capacity = max(2, 3 * part_count // (2 * devices))
    weighted = (basis_values.astype(jnp.float32) * potential[None, :, None]).astype(jnp.bfloat16)
    group_size = math.gcd(16, part_count)
    left_groups = pair_atoms[0].reshape(part_count // group_size, group_size)
    right_groups = pair_atoms[1].reshape(part_count // group_size, group_size)

    def one_group(pair_ids):
        left_rows = basis_values[pair_ids[0]]
        right_rows = weighted[pair_ids[1]]
        return jnp.einsum(
            "pgi,pgj->pij", left_rows, right_rows, preferred_element_type=jnp.float32
        ).astype(jnp.bfloat16)

    partials = lax.map(one_group, (left_groups, right_groups)).reshape(
        part_count, block_size, block_size
    )
    target = target_device[:, 0]
    serial = jnp.arange(part_count, dtype=jnp.int32)
    earlier = (target[:, None] == target[None, :]) & (serial[None, :] < serial[:, None])
    position = jnp.sum(earlier.astype(jnp.int32), axis=1)
    slot_index = target * capacity + position
    outgoing = (
        jnp.zeros((devices * capacity, block_size, block_size), jnp.bfloat16)
        .at[slot_index]
        .set(partials)
    )
    labels = jnp.full((devices * capacity,), -1, jnp.int32).at[slot_index].set(target_block)
    incoming, arrived = (
        lax.all_to_all(outgoing, ("row", "col", "panel"), split_axis=0, concat_axis=0, tiled=True),
        lax.all_to_all(labels, ("row", "col", "panel"), split_axis=0, concat_axis=0, tiled=True),
    )
    tile_blocks = density_mask.shape[0]
    half_blocks = tile_blocks // layers
    local_count = half_blocks * tile_blocks
    one_hot = (arrived.reshape(1, -1) == jnp.arange(local_count, dtype=jnp.int32)[:, None]).astype(
        jnp.bfloat16
    )
    summed = jnp.dot(
        one_hot, incoming.reshape(-1, block_size * block_size), preferred_element_type=jnp.float32
    ).astype(jnp.bfloat16)
    half_tile = summed.reshape(half_blocks, tile_blocks, block_size, block_size).transpose(
        0, 2, 1, 3
    )
    half_tile = half_tile.reshape(half_blocks * block_size, tile_blocks * block_size)
    hamiltonian = lax.all_gather(half_tile, "panel", axis=0, tiled=True)
    density_used = masked_blocks(density, density_mask, block_size)
    inverse_used = masked_blocks(inverse_intersection, inverse_mask, block_size)
    loop_size = lax.axis_size("row")
    layer_index = lax.axis_index("panel")
    per_layer = loop_size // layers
    offset = layer_index * per_layer
    product_part = cannon_product(density_used, inverse_used, offset, per_layer)
    panel_product = of_everyone(product_part, "panel").astype(jnp.bfloat16)
    gradient_part = cannon_product(hamiltonian, panel_product, offset, per_layer)
    return sent_and_summed(gradient_part, "panel", 1)


def solution(mesh):
    placed = (
        P(("row", "col", "panel"), None, None),
        P(("row", "col", "panel")),
        P(None, ("row", "col", "panel")),
        P(("row", "col", "panel"), None),
        P(("row", "col", "panel")),
        P("row", "col"),
        P("row", "col"),
        P("row", "col"),
        P("row", "col"),
    )
    return jax.shard_map(
        local, mesh=mesh, in_specs=placed, out_specs=P("row", ("col", "panel")), check_vma=False
    )
```

profile of v0, /device:TPU:1, one launch (start us, length us, event | category | flops | bytes accessed | tf_op | source)
XLA Modules:
  0.0 506.7 jit_solution(18282766428241868119)
XLA Ops:
  1.8 4.6 collective-permute-start.10
  8.1 6.0 %collective-permute-start.7 = (bf16[256,256]{1,0:T(8,128)(2,1)S(1)}, bf16[256,256]{1,0:T(8,128)(2,1)S(1)}, u32[]{:S(2)}, u32[]{:S(2)}) collective-permute-start(bf16[256,256]{1,0:T(8,128)(2,1)S(1)} %bitcast_multiply_fusion.1), channel_id=1, source_target_pairs={{2,0},{4,2},{6,4},{8,6},{10,8},{12,10},{14,12},{0,14},{3,1},{5,3},... | collective-permute-start | bytes 393224 | tf_op jit(solution)/shard_map/ppermute | solution.py:12
  17.6 4.6 all-to-all-start
  22.2 9.3 %multiply_convert_fusion = bf16[16,2048,128]{2,1,0:T(8,128)(2,1)} fusion(bf16[16,2048,128]{2,1,0:T(8,128)(2,1)} %param.15, f32[2048]{0:T(1024)} %param.16), kind=kLoop, calls=%fused_computation.20 | loop fusion | flops 12582912 | bytes 16785408 | tf_op jit(solution)/shard_map/convert_element_type | solution.py:93
  31.5 3.5 collective-permute-start.8
  45.4 202.7 %while.38 = (s32[]{:T(128)}, bf16[8,16,128,128]{3,2,1,0:T(8,128)(2,1)}, s32[8,16]{1,0:T(8,128)S(1)}, bf16[16,2048,128]{2,1,0:T(8,128)(2,1)}, s32[8,16]{1,0:T(8,1...) while((s32[]{:T(128)}, bf16[8,16,128,128]{3,2,1,0:T(8,128)(2,1)}, s32[8,16]{1,0:T(8,128)S(1)}, ...), condition=%wide.region_3.4_spmd, body=%wide.region_2.3_spmd.sunk | while | flops 1074006144 | bytes 50865232 | solution.py:105
  45.4 8.1 %gather_fusion = bf16[16,2048,128]{2,1,0:T(8,128)(2,1)} fusion(bf16[16,2048,128]{2,1,0:T(8,128)(2,1)} %get-tuple-element.224, s32[1024]{0:T(1024)S(1)} %pad_clamp_fusion.4), kind=kCustom, calls=%fused_computation.clone.1 | custom fusion | bytes 16777280 | tf_op jit(solution)/shard_map/while/body/eval_jaxpr/gather | solution.py:99
  53.5 8.1 %gather_fusion.1 = bf16[16,2048,128]{2,1,0:T(8,128)(2,1)} fusion(bf16[16,2048,128]{2,1,0:T(8,128)(2,1)} %get-tuple-element.226, s32[1024]{0:T(1024)S(1)} %pad_clamp_fusion.5), kind=kCustom, calls=%fused_computation.1.clone.1 | custom fusion | bytes 16777280 | tf_op jit(solution)/shard_map/while/body/eval_jaxpr/gather | solution.py:100
  61.6 9.2 %fusion.41 = bf16[8,16,128,128]{3,2,1,0:T(8,128)(2,1)} fusion(bf16[8,16,128,128]{3,2,1,0:T(8,128)(2,1)} %get-tuple-element.215, s32[]{:T(128)} %get-tuple-element.214, bf16[16,2048,128]{2,1,0:T(8,128)(2,1)} %gather_fusion, bf16[16,2048,128]{2,1,0:T(8,128)(2,1)} %gather_fusion.1), kind=kOutput, calls=%fused_computation.8.clone.1 | convolution fusion | flops 1074003968 | bytes 17302016 | tf_op jit(solution)/shard_map/while/body/eval_jaxpr/pgi,pgj->pij/dot_general | solution.py:101
  70.8 8.1 %gather_fusion = bf16[16,2048,128]{2,1,0:T(8,128)(2,1)} fusion(bf16[16,2048,128]{2,1,0:T(8,128)(2,1)} %get-tuple-element.224, s32[1024]{0:T(1024)S(1)} %pad_clamp_fusion.4), kind=kCustom, calls=%fused_computation.clone.1 | custom fusion | bytes 16777280 | tf_op jit(solution)/shard_map/while/body/eval_jaxpr/gather | solution.py:99
  79.0 8.1 %gather_fusion.1 = bf16[16,2048,128]{2,1,0:T(8,128)(2,1)} fusion(bf16[16,2048,128]{2,1,0:T(8,128)(2,1)} %get-tuple-element.226, s32[1024]{0:T(1024)S(1)} %pad_clamp_fusion.5), kind=kCustom, calls=%fused_computation.1.clone.1 | custom fusion | bytes 16777280 | tf_op jit(solution)/shard_map/while/body/eval_jaxpr/gather | solution.py:100
  87.1 9.1 %fusion.41 = bf16[8,16,128,128]{3,2,1,0:T(8,128)(2,1)} fusion(bf16[8,16,128,128]{3,2,1,0:T(8,128)(2,1)} %get-tuple-element.215, s32[]{:T(128)} %get-tuple-element.214, bf16[16,2048,128]{2,1,0:T(8,128)(2,1)} %gather_fusion, bf16[16,2048,128]{2,1,0:T(8,128)(2,1)} %gather_fusion.1), kind=kOutput, calls=%fused_computation.8.clone.1 | convolution fusion | flops 1074003968 | bytes 17302016 | tf_op jit(solution)/shard_map/while/body/eval_jaxpr/pgi,pgj->pij/dot_general | solution.py:101
  96.2 8.1 %gather_fusion = bf16[16,2048,128]{2,1,0:T(8,128)(2,1)} fusion(bf16[16,2048,128]{2,1,0:T(8,128)(2,1)} %get-tuple-element.224, s32[1024]{0:T(1024)S(1)} %pad_clamp_fusion.4), kind=kCustom, calls=%fused_computation.clone.1 | custom fusion | bytes 16777280 | tf_op jit(solution)/shard_map/while/body/eval_jaxpr/gather | solution.py:99
  104.4 8.1 %gather_fusion.1 = bf16[16,2048,128]{2,1,0:T(8,128)(2,1)} fusion(bf16[16,2048,128]{2,1,0:T(8,128)(2,1)} %get-tuple-element.226, s32[1024]{0:T(1024)S(1)} %pad_clamp_fusion.5), kind=kCustom, calls=%fused_computation.1.clone.1 | custom fusion | bytes 16777280 | tf_op jit(solution)/shard_map/while/body/eval_jaxpr/gather | solution.py:100
  112.5 9.1 %fusion.41 = bf16[8,16,128,128]{3,2,1,0:T(8,128)(2,1)} fusion(bf16[8,16,128,128]{3,2,1,0:T(8,128)(2,1)} %get-tuple-element.215, s32[]{:T(128)} %get-tuple-element.214, bf16[16,2048,128]{2,1,0:T(8,128)(2,1)} %gather_fusion, bf16[16,2048,128]{2,1,0:T(8,128)(2,1)} %gather_fusion.1), kind=kOutput, calls=%fused_computation.8.clone.1 | convolution fusion | flops 1074003968 | bytes 17302016 | tf_op jit(solution)/shard_map/while/body/eval_jaxpr/pgi,pgj->pij/dot_general | solution.py:101
  121.6 8.0 %gather_fusion = bf16[16,2048,128]{2,1,0:T(8,128)(2,1)} fusion(bf16[16,2048,128]{2,1,0:T(8,128)(2,1)} %get-tuple-element.224, s32[1024]{0:T(1024)S(1)} %pad_clamp_fusion.4), kind=kCustom, calls=%fused_computation.clone.1 | custom fusion | bytes 16777280 | tf_op jit(solution)/shard_map/while/body/eval_jaxpr/gather | solution.py:99
  129.6 8.1 %gather_fusion.1 = bf16[16,2048,128]{2,1,0:T(8,128)(2,1)} fusion(bf16[16,2048,128]{2,1,0:T(8,128)(2,1)} %get-tuple-element.226, s32[1024]{0:T(1024)S(1)} %pad_clamp_fusion.5), kind=kCustom, calls=%fused_computation.1.clone.1 | custom fusion | bytes 16777280 | tf_op jit(solution)/shard_map/while/body/eval_jaxpr/gather | solution.py:100
  137.8 9.1 %fusion.41 = bf16[8,16,128,128]{3,2,1,0:T(8,128)(2,1)} fusion(bf16[8,16,128,128]{3,2,1,0:T(8,128)(2,1)} %get-tuple-element.215, s32[]{:T(128)} %get-tuple-element.214, bf16[16,2048,128]{2,1,0:T(8,128)(2,1)} %gather_fusion, bf16[16,2048,128]{2,1,0:T(8,128)(2,1)} %gather_fusion.1), kind=kOutput, calls=%fused_computation.8.clone.1 | convolution fusion | flops 1074003968 | bytes 17302016 | tf_op jit(solution)/shard_map/while/body/eval_jaxpr/pgi,pgj->pij/dot_general | solution.py:101
  146.9 8.1 %gather_fusion = bf16[16,2048,128]{2,1,0:T(8,128)(2,1)} fusion(bf16[16,2048,128]{2,1,0:T(8,128)(2,1)} %get-tuple-element.224, s32[1024]{0:T(1024)S(1)} %pad_clamp_fusion.4), kind=kCustom, calls=%fused_computation.clone.1 | custom fusion | bytes 16777280 | tf_op jit(solution)/shard_map/while/body/eval_jaxpr/gather | solution.py:99
  155.0 8.1 %gather_fusion.1 = bf16[16,2048,128]{2,1,0:T(8,128)(2,1)} fusion(bf16[16,2048,128]{2,1,0:T(8,128)(2,1)} %get-tuple-element.226, s32[1024]{0:T(1024)S(1)} %pad_clamp_fusion.5), kind=kCustom, calls=%fused_computation.1.clone.1 | custom fusion | bytes 16777280 | tf_op jit(solution)/shard_map/while/body/eval_jaxpr/gather | solution.py:100
  163.1 9.1 %fusion.41 = bf16[8,16,128,128]{3,2,1,0:T(8,128)(2,1)} fusion(bf16[8,16,128,128]{3,2,1,0:T(8,128)(2,1)} %get-tuple-element.215, s32[]{:T(128)} %get-tuple-element.214, bf16[16,2048,128]{2,1,0:T(8,128)(2,1)} %gather_fusion, bf16[16,2048,128]{2,1,0:T(8,128)(2,1)} %gather_fusion.1), kind=kOutput, calls=%fused_computation.8.clone.1 | convolution fusion | flops 1074003968 | bytes 17302016 | tf_op jit(solution)/shard_map/while/body/eval_jaxpr/pgi,pgj->pij/dot_general | solution.py:101
  172.2 8.1 %gather_fusion = bf16[16,2048,128]{2,1,0:T(8,128)(2,1)} fusion(bf16[16,2048,128]{2,1,0:T(8,128)(2,1)} %get-tuple-element.224, s32[1024]{0:T(1024)S(1)} %pad_clamp_fusion.4), kind=kCustom, calls=%fused_computation.clone.1 | custom fusion | bytes 16777280 | tf_op jit(solution)/shard_map/while/body/eval_jaxpr/gather | solution.py:99
  180.3 8.1 %gather_fusion.1 = bf16[16,2048,128]{2,1,0:T(8,128)(2,1)} fusion(bf16[16,2048,128]{2,1,0:T(8,128)(2,1)} %get-tuple-element.226, s32[1024]{0:T(1024)S(1)} %pad_clamp_fusion.5), kind=kCustom, calls=%fused_computation.1.clone.1 | custom fusion | bytes 16777280 | tf_op jit(solution)/shard_map/while/body/eval_jaxpr/gather | solution.py:100
  188.4 9.1 %fusion.41 = bf16[8,16,128,128]{3,2,1,0:T(8,128)(2,1)} fusion(bf16[8,16,128,128]{3,2,1,0:T(8,128)(2,1)} %get-tuple-element.215, s32[]{:T(128)} %get-tuple-element.214, bf16[16,2048,128]{2,1,0:T(8,128)(2,1)} %gather_fusion, bf16[16,2048,128]{2,1,0:T(8,128)(2,1)} %gather_fusion.1), kind=kOutput, calls=%fused_computation.8.clone.1 | convolution fusion | flops 1074003968 | bytes 17302016 | tf_op jit(solution)/shard_map/while/body/eval_jaxpr/pgi,pgj->pij/dot_general | solution.py:101
  197.5 8.1 %gather_fusion = bf16[16,2048,128]{2,1,0:T(8,128)(2,1)} fusion(bf16[16,2048,128]{2,1,0:T(8,128)(2,1)} %get-tuple-element.224, s32[1024]{0:T(1024)S(1)} %pad_clamp_fusion.4), kind=kCustom, calls=%fused_computation.clone.1 | custom fusion | bytes 16777280 | tf_op jit(solution)/shard_map/while/body/eval_jaxpr/gather | solution.py:99
  205.7 8.1 %gather_fusion.1 = bf16[16,2048,128]{2,1,0:T(8,128)(2,1)} fusion(bf16[16,2048,128]{2,1,0:T(8,128)(2,1)} %get-tuple-element.226, s32[1024]{0:T(1024)S(1)} %pad_clamp_fusion.5), kind=kCustom, calls=%fused_computation.1.clone.1 | custom fusion | bytes 16777280 | tf_op jit(solution)/shard_map/while/body/eval_jaxpr/gather | solution.py:100
  213.7 9.1 %fusion.41 = bf16[8,16,128,128]{3,2,1,0:T(8,128)(2,1)} fusion(bf16[8,16,128,128]{3,2,1,0:T(8,128)(2,1)} %get-tuple-element.215, s32[]{:T(128)} %get-tuple-element.214, bf16[16,2048,128]{2,1,0:T(8,128)(2,1)} %gather_fusion, bf16[16,2048,128]{2,1,0:T(8,128)(2,1)} %gather_fusion.1), kind=kOutput, calls=%fused_computation.8.clone.1 | convolution fusion | flops 1074003968 | bytes 17302016 | tf_op jit(solution)/shard_map/while/body/eval_jaxpr/pgi,pgj->pij/dot_general | solution.py:101
  222.8 8.1 %gather_fusion = bf16[16,2048,128]{2,1,0:T(8,128)(2,1)} fusion(bf16[16,2048,128]{2,1,0:T(8,128)(2,1)} %get-tuple-element.224, s32[1024]{0:T(1024)S(1)} %pad_clamp_fusion.4), kind=kCustom, calls=%fused_computation.clone.1 | custom fusion | bytes 16777280 | tf_op jit(solution)/shard_map/while/body/eval_jaxpr/gather | solution.py:99
  231.0 8.1 %gather_fusion.1 = bf16[16,2048,128]{2,1,0:T(8,128)(2,1)} fusion(bf16[16,2048,128]{2,1,0:T(8,128)(2,1)} %get-tuple-element.226, s32[1024]{0:T(1024)S(1)} %pad_clamp_fusion.5), kind=kCustom, calls=%fused_computation.1.clone.1 | custom fusion | bytes 16777280 | tf_op jit(solution)/shard_map/while/body/eval_jaxpr/gather | solution.py:100
  239.0 9.1 %fusion.41 = bf16[8,16,128,128]{3,2,1,0:T(8,128)(2,1)} fusion(bf16[8,16,128,128]{3,2,1,0:T(8,128)(2,1)} %get-tuple-element.215, s32[]{:T(128)} %get-tuple-element.214, bf16[16,2048,128]{2,1,0:T(8,128)(2,1)} %gather_fusion, bf16[16,2048,128]{2,1,0:T(8,128)(2,1)} %gather_fusion.1), kind=kOutput, calls=%fused_computation.8.clone.1 | convolution fusion | flops 1074003968 | bytes 17302016 | tf_op jit(solution)/shard_map/while/body/eval_jaxpr/pgi,pgj->pij/dot_general | solution.py:101
  248.1 5.3 %broadcast_in_dim.15 = bf16[256,128,128]{2,1,0:T(8,128)(2,1)} broadcast(bf16[]{:T(256)} %constant.109.clone.1), dimensions={} | broadcast | bytes 8388610 | tf_op jit(solution)/shard_map/broadcast_in_dim | solution.py:114
  253.5 19.6 %scatter_fusion = bf16[256,128,128]{2,1,0:T(8,128)(2,1)} fusion(bf16[256,128,128]{2,1,0:T(8,128)(2,1)} %broadcast_in_dim.15, s32[128]{0:T(128)S(1)} %fusion.15, bf16[128,128,128]{2,1,0:T(8,128)(2,1)} %bitcast.89), kind=kCustom, calls=%fused_computation.3 | custom fusion | bytes 12583424 | tf_op jit(solution)/shard_map/scatter | solution.py:116
  273.4 28.8 %while.39 = (s32[]{:T(128)}, f32[256,512]{1,0:T(8,128)S(1)}, bf16[256,256]{1,0:T(8,128)(2,1)S(1)}, bf16[256,512]{1,0:T(8,128)(2,1)S(1)}, s32[]{:T(128)}) while((s32[]{:T(128)}, f32[256,512]{1,0:T(8,128)S(1)}, bf16[256,256]{1,0:T(8,128)(2,1)S(1)}, bf16[256,512]{1,0:T(8,128)(2,1)S(1)}, s32[]{:T(128)}) %tuple.51), condition=%wide.region_6.7_spmd, body=%wide.region_5.6_spmd.sunk | while | flops 67239936 | bytes 3801229 | solution.py:71
  278.1 6.9 %collective-permute-done = bf16[256,256]{1,0:T(8,128)(2,1)S(1)} collective-permute-done((bf16[256,256]{1,0:T(8,128)(2,1)S(1)}, bf16[256,256]{1,0:T(8,128)(2,1)S(1)}, u32[]{:S(2)}, u32[]{:S(2)}) %collective-permute-start) | collective-permute-done | bytes 131104 | tf_op jit(solution)/shard_map/while/body/eval_jaxpr/ppermute | solution.py:12
  293.7 5.1 collective-permute-start
  302.2 9.8 %all_to_all.24 = f32[2,256,512]{2,1,0:T(8,128)S(1)} all-to-all(f32[2,256,512]{2,1,0:T(8,128)S(1)} %broadcast_in_dim.17), channel_id=1, replica_groups=mesh['row'=8,'col'=8,'panel'=2] {'panel'}, dimensions={0} | all-to-all | bytes 2097152 | tf_op jit(solution)/shard_map/all_to_all | solution.py:17
  312.0 9.8 %all-to-all-start.1 = ((bf16[256,128,128]{2,1,0:T(8,128)(2,1)}), bf16[256,128,128]{2,1,0:T(8,128)(2,1)}, u32[]{:S(2)}, u32[]{:S(2)}) async-start(bf16[256,128,128]{2,1,0:T(8,128)(2,1)} %scatter_fusion), calls=%async_computation.1 | async-start | bytes 16777216 | tf_op jit(solution)/shard_map/all_to_all | solution.py:120
  323.4 3.9 collective-permute-start.13
  327.3 94.4 %all-to-all-done.1 = bf16[256,128,128]{2,1,0:T(8,128)(2,1)} async-done(((bf16[256,128,128]{2,1,0:T(8,128)(2,1)}), bf16[256,128,128]{2,1,0:T(8,128)(2,1)}, u32[]{:S(2)}, u32[]{:S(2)}) %all-to-all-start.1) | async-done | bytes 8388640 | tf_op jit(solution)/shard_map/all_to_all | solution.py:120
  421.7 7.9 %fusion.8 = bf16[1,2,128,128]{3,1,2,0:T(2,128)(2,1)S(1)} fusion(bf16[32,8,128,128]{3,2,1,0:T(8,128)(2,1)} %bitcast.14, s32[256]{0:T(256)S(1)} %eq.78), kind=kOutput, calls=%fused_computation.23 | convolution fusion | flops 16810496 | bytes 8455168 | tf_op jit(solution)/shard_map/dot_general | solution.py:129
  432.6 5.2 %collective-permute-start.4 = (bf16[256,256]{1,0:T(8,128)(2,1)S(1)}, bf16[256,256]{1,0:T(8,128)(2,1)S(1)}, u32[]{:S(2)}, u32[]{:S(2)}) collective-permute-start(bf16[256,256]{1,0:T(8,128)(2,1)S(1)} %all_gather.3), channel_id=1, source_target_pairs={{2,0},{4,2},{6,4},{8,6},{10,8},{12,10},{14,12},{0,14},{3,1},{5,3},... | collective-permute-start | bytes 393224 | tf_op jit(solution)/shard_map/ppermute | solution.py:12
  449.1 4.2 collective-permute-done.15
  454.3 41.7 %while.40 = (s32[]{:T(128)}, f32[256,512]{1,0:T(8,128)S(1)}, bf16[256,256]{1,0:T(8,128)(2,1)S(1)}, bf16[256,512]{1,0:T(8,128)(2,1)S(1)}, s32[]{:T(128)}) while((s32[]{:T(128)}, f32[256,512]{1,0:T(8,128)S(1)}, bf16[256,256]{1,0:T(8,128)(2,1)S(1)}, bf16[256,512]{1,0:T(8,128)(2,1)S(1)}, s32[]{:T(128)}) %tuple.54), condition=%wide.region_9.10_spmd, body=%wide.region_8.9_spmd.sunk | while | flops 67239936 | bytes 3801229 | solution.py:71
  454.3 16.2 %collective-permute-start.3 = (bf16[256,512]{1,0:T(8,128)(2,1)S(1)}, bf16[256,512]{1,0:T(8,128)(2,1)S(1)}, u32[]{:S(2)}, u32[]{:S(2)}) collective-permute-start(bf16[256,512]{1,0:T(8,128)(2,1)S(1)} %get-tuple-element.251), channel_id=1, source_target_pairs={{16,0},{32,16},{48,32},{64,48},{80,64},{96,80},{112,96},{0,112},{1... | collective-permute-start | bytes 786440 | tf_op jit(solution)/shard_map/while/body/eval_jaxpr/ppermute | solution.py:12
  471.1 6.2 %collective-permute-done.2 = bf16[256,256]{1,0:T(8,128)(2,1)S(1)} collective-permute-done((bf16[256,256]{1,0:T(8,128)(2,1)S(1)}, bf16[256,256]{1,0:T(8,128)(2,1)S(1)}, u32[]{:S(2)}, u32[]{:S(2)}) %collective-permute-start.2) | collective-permute-done | bytes 131104 | tf_op jit(solution)/shard_map/while/body/eval_jaxpr/ppermute | solution.py:12
  478.9 4.9 collective-permute-start.2
  487.6 5.6 %collective-permute-start.2 = (bf16[256,256]{1,0:T(8,128)(2,1)S(1)}, bf16[256,256]{1,0:T(8,128)(2,1)S(1)}, u32[]{:S(2)}, u32[]{:S(2)}) collective-permute-start(bf16[256,256]{1,0:T(8,128)(2,1)S(1)} %get-tuple-element.250), channel_id=1, source_target_pairs={{2,0},{4,2},{6,4},{8,6},{10,8},{12,10},{14,12},{0,14},{3,1},{5,3},... | collective-permute-start | bytes 393224 | tf_op jit(solution)/shard_map/while/body/eval_jaxpr/ppermute | solution.py:12
  496.4 9.5 %all_to_all.25 = f32[2,256,256]{2,1,0:T(8,128)S(1)} all-to-all(f32[2,256,256]{2,1,0:T(8,128)S(1)} %copy.26), channel_id=1, replica_groups=mesh['row'=8,'col'=8,'panel'=2] {'panel'}, dimensions={0} | all-to-all | bytes 1048576 | tf_op jit(solution)/shard_map/all_to_all | solution.py:33
  (121 shorter events, 61.3 us)
Async XLA Ops:
  1.8 33.2 %collective-permute-start.10 = (bf16[256,512]{1,0:T(8,128)(2,1)S(1)}, bf16[256,512]{1,0:T(8,128)(2,1)S(1)}, u32[]{:S(2)}, u32[]{:S(2)}) collective-permute-start(bf16[256,512]{1,0:T(8,128)(2,1)S(1)} %bitcast_multiply_fusion), channel_id=1, source_target_pairs={{16,0},{32,16},{48,32},{64,48},{80,64},{96,80},{112,96},{0,112},{1... | collective-permute-start | bytes 786440 | tf_op jit(solution)/shard_map/ppermute | solution.py:12
  8.1 23.4 %collective-permute-start.7 = (bf16[256,256]{1,0:T(8,128)(2,1)S(1)}, bf16[256,256]{1,0:T(8,128)(2,1)S(1)}, u32[]{:S(2)}, u32[]{:S(2)}) collective-permute-start(bf16[256,256]{1,0:T(8,128)(2,1)S(1)} %bitcast_multiply_fusion.1), channel_id=1, source_target_pairs={{2,0},{4,2},{6,4},{8,6},{10,8},{12,10},{14,12},{0,14},{3,1},{5,3},... | collective-permute-start | bytes 393224 | tf_op jit(solution)/shard_map/ppermute | solution.py:12
  17.6 255.8 %all-to-all-start = ((s32[128,2,1]{1,2,0:T(1,128)}), s32[128,2,1]{1,2,0:T(1,128)S(1)}, u32[]{:S(2)}, u32[]{:S(2)}) async-start(s32[128,2,1]{1,2,0:T(1,128)} %bitcast.8), calls=%async_computation | async-start | bytes 131072 | tf_op jit(solution)/shard_map/all_to_all | solution.py:121
  22.2 15.5 %copy-start = (s32[2,128]{1,0:T(2,128)S(1)}, s32[2,128]{1,0:T(2,128)}, u32[]{:S(2)}) copy-start(s32[2,128]{1,0:T(2,128)} %param.17) | copy-start | bytes 3076
  31.5 6.4 %collective-permute-start.8 = (bf16[256,256]{1,0:T(8,128)(2,1)S(1)}, bf16[256,256]{1,0:T(8,128)(2,1)S(1)}, u32[]{:S(2)}, u32[]{:S(2)}) collective-permute-start(bf16[256,256]{1,0:T(8,128)(2,1)S(1)} %broadcast_select_fusion.6), channel_id=1, source_target_pairs={{4,0},{6,2},{8,4},{10,6},{12,8},{14,10},{0,12},{2,14},{5,1},{7,3},... | collective-permute-start | bytes 393224 | tf_op jit(solution)/shard_map/ppermute | solution.py:12
  35.0 7.7 %collective-permute-start.11 = (bf16[256,512]{1,0:T(8,128)(2,1)S(1)}, bf16[256,512]{1,0:T(8,128)(2,1)S(1)}, u32[]{:S(2)}, u32[]{:S(2)}) collective-permute-start(bf16[256,512]{1,0:T(8,128)(2,1)S(1)} %broadcast_select_fusion.1), channel_id=1, source_target_pairs={{32,0},{48,16},{64,32},{80,48},{96,64},{112,80},{0,96},{16,112},{3... | collective-permute-start | bytes 786440 | tf_op jit(solution)/shard_map/ppermute | solution.py:12
  38.0 235.1 %collective-permute-start.9 = (bf16[256,256]{1,0:T(8,128)(2,1)S(1)}, bf16[256,256]{1,0:T(8,128)(2,1)S(1)}, u32[]{:S(2)}, u32[]{:S(2)}) collective-permute-start(bf16[256,256]{1,0:T(8,128)(2,1)S(1)} %broadcast_select_fusion.8), channel_id=1, source_target_pairs={{8,0},{10,2},{12,4},{14,6},{0,8},{2,10},{4,12},{6,14},{9,1},{11,3}... | collective-permute-start | bytes 393224 | tf_op jit(solution)/shard_map/ppermute | solution.py:12
  42.7 230.3 %collective-permute-start.12 = (bf16[256,512]{1,0:T(8,128)(2,1)S(1)}, bf16[256,512]{1,0:T(8,128)(2,1)S(1)}, u32[]{:S(2)}, u32[]{:S(2)}) collective-permute-start(bf16[256,512]{1,0:T(8,128)(2,1)S(1)} %broadcast_select_fusion.3), channel_id=1, source_target_pairs={{64,0},{80,16},{96,32},{112,48},{0,64},{16,80},{32,96},{48,112},{6... | collective-permute-start | bytes 786440 | tf_op jit(solution)/shard_map/ppermute | solution.py:12
  273.4 11.7 %collective-permute-start.1 = (bf16[256,512]{1,0:T(8,128)(2,1)S(1)}, bf16[256,512]{1,0:T(8,128)(2,1)S(1)}, u32[]{:S(2)}, u32[]{:S(2)}) collective-permute-start(bf16[256,512]{1,0:T(8,128)(2,1)S(1)} %get-tuple-element.236), channel_id=1, source_target_pairs={{16,0},{32,16},{48,32},{64,48},{80,64},{96,80},{112,96},{0,112},{1... | collective-permute-start | bytes 786440 | tf_op jit(solution)/shard_map/while/body/eval_jaxpr/ppermute | solution.py:12
  275.6 9.5 %collective-permute-start = (bf16[256,256]{1,0:T(8,128)(2,1)S(1)}, bf16[256,256]{1,0:T(8,128)(2,1)S(1)}, u32[]{:S(2)}, u32[]{:S(2)}) collective-permute-start(bf16[256,256]{1,0:T(8,128)(2,1)S(1)} %get-tuple-element.235), channel_id=1, source_target_pairs={{2,0},{4,2},{6,4},{8,6},{10,8},{12,10},{14,12},{0,14},{3,1},{5,3},... | collective-permute-start | bytes 393224 | tf_op jit(solution)/shard_map/while/body/eval_jaxpr/ppermute | solution.py:12
  285.3 7.3 %collective-permute-start.1 = (bf16[256,512]{1,0:T(8,128)(2,1)S(1)}, bf16[256,512]{1,0:T(8,128)(2,1)S(1)}, u32[]{:S(2)}, u32[]{:S(2)}) collective-permute-start(bf16[256,512]{1,0:T(8,128)(2,1)S(1)} %get-tuple-element.236), channel_id=1, source_target_pairs={{16,0},{32,16},{48,32},{64,48},{80,64},{96,80},{112,96},{0,112},{1... | collective-permute-start | bytes 786440 | tf_op jit(solution)/shard_map/while/body/eval_jaxpr/ppermute | solution.py:12
  286.1 6.5 %collective-permute-start = (bf16[256,256]{1,0:T(8,128)(2,1)S(1)}, bf16[256,256]{1,0:T(8,128)(2,1)S(1)}, u32[]{:S(2)}, u32[]{:S(2)}) collective-permute-start(bf16[256,256]{1,0:T(8,128)(2,1)S(1)} %get-tuple-element.235), channel_id=1, source_target_pairs={{2,0},{4,2},{6,4},{8,6},{10,8},{12,10},{14,12},{0,14},{3,1},{5,3},... | collective-permute-start | bytes 393224 | tf_op jit(solution)/shard_map/while/body/eval_jaxpr/ppermute | solution.py:12
  292.9 8.9 %collective-permute-start.1 = (bf16[256,512]{1,0:T(8,128)(2,1)S(1)}, bf16[256,512]{1,0:T(8,128)(2,1)S(1)}, u32[]{:S(2)}, u32[]{:S(2)}) collective-permute-start(bf16[256,512]{1,0:T(8,128)(2,1)S(1)} %get-tuple-element.236), channel_id=1, source_target_pairs={{16,0},{32,16},{48,32},{64,48},{80,64},{96,80},{112,96},{0,112},{1... | collective-permute-start | bytes 786440 | tf_op jit(solution)/shard_map/while/body/eval_jaxpr/ppermute | solution.py:12
  293.7 8.1 %collective-permute-start = (bf16[256,256]{1,0:T(8,128)(2,1)S(1)}, bf16[256,256]{1,0:T(8,128)(2,1)S(1)}, u32[]{:S(2)}, u32[]{:S(2)}) collective-permute-start(bf16[256,256]{1,0:T(8,128)(2,1)S(1)} %get-tuple-element.235), channel_id=1, source_target_pairs={{2,0},{4,2},{6,4},{8,6},{10,8},{12,10},{14,12},{0,14},{3,1},{5,3},... | collective-permute-start | bytes 393224 | tf_op jit(solution)/shard_map/while/body/eval_jaxpr/ppermute | solution.py:12
  312.0 109.7 %all-to-all-start.1 = ((bf16[256,128,128]{2,1,0:T(8,128)(2,1)}), bf16[256,128,128]{2,1,0:T(8,128)(2,1)}, u32[]{:S(2)}, u32[]{:S(2)}) async-start(bf16[256,128,128]{2,1,0:T(8,128)(2,1)} %scatter_fusion), calls=%async_computation.1 | async-start | bytes 16777216 | tf_op jit(solution)/shard_map/all_to_all | solution.py:120
  323.4 114.4 %collective-permute-start.13 = (bf16[256,512]{1,0:T(8,128)(2,1)S(1)}, bf16[256,512]{1,0:T(8,128)(2,1)S(1)}, u32[]{:S(2)}, u32[]{:S(2)}) collective-permute-start(bf16[256,512]{1,0:T(8,128)(2,1)S(1)} %reduce_sum.31), channel_id=1, source_target_pairs={{16,0},{32,16},{48,32},{64,48},{80,64},{96,80},{112,96},{0,112},{1... | collective-permute-start | bytes 786440 | tf_op jit(solution)/shard_map/ppermute | solution.py:12
  432.6 7.9 %collective-permute-start.4 = (bf16[256,256]{1,0:T(8,128)(2,1)S(1)}, bf16[256,256]{1,0:T(8,128)(2,1)S(1)}, u32[]{:S(2)}, u32[]{:S(2)}) collective-permute-start(bf16[256,256]{1,0:T(8,128)(2,1)S(1)} %all_gather.3), channel_id=1, source_target_pairs={{2,0},{4,2},{6,4},{8,6},{10,8},{12,10},{14,12},{0,14},{3,1},{5,3},... | collective-permute-start | bytes 393224 | tf_op jit(solution)/shard_map/ppermute | solution.py:12
  437.9 7.3 %collective-permute-start.14 = (bf16[256,512]{1,0:T(8,128)(2,1)S(1)}, bf16[256,512]{1,0:T(8,128)(2,1)S(1)}, u32[]{:S(2)}, u32[]{:S(2)}) collective-permute-start(bf16[256,512]{1,0:T(8,128)(2,1)S(1)} %broadcast_select_fusion), channel_id=1, source_target_pairs={{32,0},{48,16},{64,32},{80,48},{96,64},{112,80},{0,96},{16,112},{3... | collective-permute-start | bytes 786440 | tf_op jit(solution)/shard_map/ppermute | solution.py:12
  440.6 7.8 %collective-permute-start.5 = (bf16[256,256]{1,0:T(8,128)(2,1)S(1)}, bf16[256,256]{1,0:T(8,128)(2,1)S(1)}, u32[]{:S(2)}, u32[]{:S(2)}) collective-permute-start(bf16[256,256]{1,0:T(8,128)(2,1)S(1)} %broadcast_select_fusion.7), channel_id=1, source_target_pairs={{4,0},{6,2},{8,4},{10,6},{12,8},{14,10},{0,12},{2,14},{5,1},{7,3},... | collective-permute-start | bytes 393224 | tf_op jit(solution)/shard_map/ppermute | solution.py:12
  445.2 8.1 %collective-permute-start.15 = (bf16[256,512]{1,0:T(8,128)(2,1)S(1)}, bf16[256,512]{1,0:T(8,128)(2,1)S(1)}, u32[]{:S(2)}, u32[]{:S(2)}) collective-permute-start(bf16[256,512]{1,0:T(8,128)(2,1)S(1)} %broadcast_select_fusion.2), channel_id=1, source_target_pairs={{64,0},{80,16},{96,32},{112,48},{0,64},{16,80},{32,96},{48,112},{6... | collective-permute-start | bytes 786440 | tf_op jit(solution)/shard_map/ppermute | solution.py:12
  448.3 5.7 %collective-permute-start.6 = (bf16[256,256]{1,0:T(8,128)(2,1)S(1)}, bf16[256,256]{1,0:T(8,128)(2,1)S(1)}, u32[]{:S(2)}, u32[]{:S(2)}) collective-permute-start(bf16[256,256]{1,0:T(8,128)(2,1)S(1)} %broadcast_select_fusion.9), channel_id=1, source_target_pairs={{8,0},{10,2},{12,4},{14,6},{0,8},{2,10},{4,12},{6,14},{9,1},{11,3}... | collective-permute-start | bytes 393224 | tf_op jit(solution)/shard_map/ppermute | solution.py:12
  454.3 23.0 %collective-permute-start.3 = (bf16[256,512]{1,0:T(8,128)(2,1)S(1)}, bf16[256,512]{1,0:T(8,128)(2,1)S(1)}, u32[]{:S(2)}, u32[]{:S(2)}) collective-permute-start(bf16[256,512]{1,0:T(8,128)(2,1)S(1)} %get-tuple-element.251), channel_id=1, source_target_pairs={{16,0},{32,16},{48,32},{64,48},{80,64},{96,80},{112,96},{0,112},{1... | collective-permute-start | bytes 786440 | tf_op jit(solution)/shard_map/while/body/eval_jaxpr/ppermute | solution.py:12
  470.6 6.7 %collective-permute-start.2 = (bf16[256,256]{1,0:T(8,128)(2,1)S(1)}, bf16[256,256]{1,0:T(8,128)(2,1)S(1)}, u32[]{:S(2)}, u32[]{:S(2)}) collective-permute-start(bf16[256,256]{1,0:T(8,128)(2,1)S(1)} %get-tuple-element.250), channel_id=1, source_target_pairs={{2,0},{4,2},{6,4},{8,6},{10,8},{12,10},{14,12},{0,14},{3,1},{5,3},... | collective-permute-start | bytes 393224 | tf_op jit(solution)/shard_map/while/body/eval_jaxpr/ppermute | solution.py:12
  477.6 9.6 %collective-permute-start.3 = (bf16[256,512]{1,0:T(8,128)(2,1)S(1)}, bf16[256,512]{1,0:T(8,128)(2,1)S(1)}, u32[]{:S(2)}, u32[]{:S(2)}) collective-permute-start(bf16[256,512]{1,0:T(8,128)(2,1)S(1)} %get-tuple-element.251), channel_id=1, source_target_pairs={{16,0},{32,16},{48,32},{64,48},{80,64},{96,80},{112,96},{0,112},{1... | collective-permute-start | bytes 786440 | tf_op jit(solution)/shard_map/while/body/eval_jaxpr/ppermute | solution.py:12
  478.9 8.3 %collective-permute-start.2 = (bf16[256,256]{1,0:T(8,128)(2,1)S(1)}, bf16[256,256]{1,0:T(8,128)(2,1)S(1)}, u32[]{:S(2)}, u32[]{:S(2)}) collective-permute-start(bf16[256,256]{1,0:T(8,128)(2,1)S(1)} %get-tuple-element.250), channel_id=1, source_target_pairs={{2,0},{4,2},{6,4},{8,6},{10,8},{12,10},{14,12},{0,14},{3,1},{5,3},... | collective-permute-start | bytes 393224 | tf_op jit(solution)/shard_map/while/body/eval_jaxpr/ppermute | solution.py:12
  487.5 8.2 %collective-permute-start.3 = (bf16[256,512]{1,0:T(8,128)(2,1)S(1)}, bf16[256,512]{1,0:T(8,128)(2,1)S(1)}, u32[]{:S(2)}, u32[]{:S(2)}) collective-permute-start(bf16[256,512]{1,0:T(8,128)(2,1)S(1)} %get-tuple-element.251), channel_id=1, source_target_pairs={{16,0},{32,16},{48,32},{64,48},{80,64},{96,80},{112,96},{0,112},{1... | collective-permute-start | bytes 786440 | tf_op jit(solution)/shard_map/while/body/eval_jaxpr/ppermute | solution.py:12
  487.6 8.1 %collective-permute-start.2 = (bf16[256,256]{1,0:T(8,128)(2,1)S(1)}, bf16[256,256]{1,0:T(8,128)(2,1)S(1)}, u32[]{:S(2)}, u32[]{:S(2)}) collective-permute-start(bf16[256,256]{1,0:T(8,128)(2,1)S(1)} %get-tuple-element.250), channel_id=1, source_target_pairs={{2,0},{4,2},{6,4},{8,6},{10,8},{12,10},{14,12},{0,14},{3,1},{5,3},... | collective-permute-start | bytes 393224 | tf_op jit(solution)/shard_map/while/body/eval_jaxpr/ppermute | solution.py:12
where the time goes:
time: 508 us; the launch traced here: 507 us
  local copies, waits for them, and re-layouts  158 us (31%)
  waiting for transfers between devices  132 us (26%)
  starting transfers between devices  95 us (19%)
  matrix products  82.6 us (16%)
  blocking collectives  22.3 us (4%)
  other arithmetic  16.2 us (3%)
    all_to_all x1, waiting for transfers between devices, local(): lax.all_to_all(outgoing, ('row', 'col', 'panel'), split_axis=0, concat_ax...  94.4 us
    ppermute x24, starting transfers between devices, shifted_2(): return lax.ppermute(block, axis, route)  80.6 us
    dot_general x8, matrix products, one_group(): jnp.einsum('pgi,pgj->pij', left_rows, right_rows, preferred_element_type=...  72.8 us
    gather x8, local copies, waits for them, and re-layouts, one_group(): left_rows = basis_values[pair_ids[0]]  64.9 us
    gather x8, local copies, waits for them, and re-layouts, one_group(): right_rows = weighted[pair_ids[1]]  64.8 us
    ppermute x24, waiting for transfers between devices, shifted_2(): return lax.ppermute(block, axis, route)  37.3 us
    scatter x1, local copies, waits for them, and re-layouts, local(): outgoing = jnp.zeros((devices * capacity, block_size, block_size), jnp.bf...  19.6 us
  transfers between devices with their start and end apart: 26, of which 12 were waited for; matrix products, arithmetic and copies ran while one was open for 50% of the time, Pallas kernels for 0%

commit v1 on v0

v1 whole, which is shorter than its diff:
```python
import functools

import jax
import jax.numpy as jnp
from jax import lax
from jax.experimental import pallas as pl
from jax.experimental.pallas import tpu as pltpu
from jax.sharding import PartitionSpec as P

ALL = ("row", "col", "panel")


def masked_blocks(matrix, block_mask, block_size):
    mask_rows, mask_cols = block_mask.shape
    shaped = matrix.reshape(mask_rows, block_size, mask_cols, block_size)
    factor = block_mask.astype(matrix.dtype)[:, None, :, None]
    return (shaped * factor).reshape(mask_rows * block_size, mask_cols * block_size)


SIZE = 128
SHARES = (48, 48, 32)
STARTS = (0, 48, 96)
ORDERS = (("x", "y", "z"), ("y", "z", "x"), ("z", "x", "y"))


def gram_kernel(first_ref, second_ref, weight_ref, basis_ref, out0, out1, out2, raw, left, right, blocks, column, sem):
    atoms, points, size = basis_ref.shape
    chunks = points // size

    def fetch(a):
        return pltpu.make_async_copy(basis_ref.at[a], raw.at[a], sem.at[a])

    for a in range(atoms):
        fetch(a).start()
    for k in range(chunks):
        spread = jnp.broadcast_to(weight_ref[k : k + 1, :], (size, size))
        column[k * size : (k + 1) * size, :] = spread.T
    blocks[atoms * atoms] = jnp.zeros((size, size), jnp.bfloat16)
    for a in range(atoms):
        fetch(a).wait()

        @pl.loop(0, chunks)
        def _(k):
            rows = pl.ds(pl.multiple_of(k * size, size), size)
            piece = raw[a, rows, :]
            left[pl.ds(a * size, size), rows] = piece.T
            scaled = piece.astype(jnp.float32) * column[rows, :]
            right[rows, pl.ds(a * size, size)] = scaled.astype(jnp.bfloat16)

    tall, wide = 4, 2

    @pl.loop(0, (atoms // tall) * (atoms // wide))
    def _(t):
        i, j = t // (atoms // wide), t % (atoms // wide)
        rows = pl.ds(pl.multiple_of(i * tall * size, tall * size), tall * size)
        cols = pl.ds(pl.multiple_of(j * wide * size, wide * size), wide * size)
        product = jnp.dot(left[rows, :], right[:, cols], preferred_element_type=jnp.float32)
        for u in range(tall):
            for v in range(wide):
                part = product[u * size : (u + 1) * size, v * size : (v + 1) * size]
                blocks[(i * tall + u) * atoms + j * wide + v] = part.astype(jnp.bfloat16)

    @pl.loop(0, first_ref.shape[0])
    def _(n):
        y, x_lo, z, x_hi, p, b = n // 64, n // 32 % 2, n // 8 % 4, n // 4 % 2, n // 2 % 2, n % 2
        at = {"x": x_hi * 2 + x_lo, "y": y, "z": z}
        total = blocks[first_ref[n]] + blocks[second_ref[n]]
        for out, order, start, share in zip((out0, out1, out2), ORDERS, STARTS, SHARES):
            d0, d1, d2 = (at[axis] for axis in order)
            out[p, d0, (d1 * 4 + d2) * 2 + b] = total[start : start + share, :]


def gram_blocks(first, second, weights, basis):
    atoms, points, size = basis.shape
    vmem = pl.BlockSpec(memory_space=pltpu.VMEM)
    smem = pl.BlockSpec(memory_space=pltpu.SMEM)
    return pl.pallas_call(
        gram_kernel,
        out_shape=[jax.ShapeDtypeStruct((2, 4, 32, share, size), jnp.bfloat16) for share in SHARES],
        in_specs=[smem, smem, vmem, pl.BlockSpec(memory_space=pl.ANY)],
        out_specs=[vmem] * 3,
        scratch_shapes=[
            pltpu.VMEM((atoms, points, size), jnp.bfloat16),
            pltpu.VMEM((atoms * size, points), jnp.bfloat16),
            pltpu.VMEM((points, atoms * size), jnp.bfloat16),
            pltpu.VMEM((atoms * atoms + 1, size, size), jnp.bfloat16),
            pltpu.VMEM((points, size), jnp.float32),
            pltpu.SemaphoreType.DMA((atoms,)),
        ],
        compiler_params=pltpu.CompilerParams(vmem_limit_bytes=56 << 20),
        cost_estimate=pl.CostEstimate(
            flops=2 * (atoms * size) ** 2 * points, bytes_accessed=20 << 20, transcendentals=0
        ),
    )(first, second, weights.reshape(-1, size), basis)


def place():
    row, col, core = (lax.axis_index(axis) for axis in ALL)
    return {"x": col % 2 * 2 + row % 2, "y": row // 2, "z": col // 2, "core": core}


def device_at(spot):
    return (spot["y"] * 2 + spot["x"] % 2, spot["z"] * 2 + spot["x"] // 2, spot["core"])


def moved(spot, axis, steps):
    return {**spot, axis: (spot[axis] + steps) % (2 if axis == "core" else 4)}


def reduce_kernel(
    in0, in1, in2, out_ref,
    own0, own1, own2, pair0, pair1, pair2,
    got10, got11, got12, one0, one1, one2,
    got20, got21, got22, two0, two1, two2,
    got30, got31, got32, row_buf,
    load_sem, pair_send, pair_recv, send_sem, recv_sem, gather_send, gather_recv, share_send, share_recv, out_sem,
):
    here = place()
    ins, own, pair = (in0, in1, in2), (own0, own1, own2), (pair0, pair1, pair2)
    sources = (own, (one0, one1, one2), (two0, two1, two2))
    lands = ((got10, got11, got12), (got20, got21, got22), (got30, got31, got32))
    partner = moved(here, "core", 1)
    mesh = pl.DeviceIdType.MESH

    peers = [partner]
    for axis in ("x", "y", "z"):
        peers += [moved(here, axis, d) for d in (1, 2, 3)]
    peers += [moved(moved(here, "x", 2), "z", d) for d in (1, 2, 3)]
    barrier = pltpu.get_barrier_semaphore()
    for peer in peers:
        pl.semaphore_signal(barrier, inc=1, device_id=device_at(peer), device_id_type=mesh)
    pl.semaphore_wait(barrier, len(peers))

    def load(k, d):
        q = (here[ORDERS[k][0]] + d) % 4
        return pltpu.make_async_copy(ins[k].at[here["core"], q], own[k].at[q], load_sem.at[k, d])

    def swap(k, d):
        q = (here[ORDERS[k][0]] + d) % 4
        return pltpu.make_async_remote_copy(
            ins[k].at[partner["core"], q], pair[k].at[q], pair_send.at[k, d], pair_recv.at[k, d],
            device_id=device_at(partner), device_id_type=mesh,
        )

    def pass_on(stage, k, d):
        axis = ORDERS[k][stage]
        return pltpu.make_async_remote_copy(
            sources[stage][k].at[(here[axis] + d) % 4], lands[stage][k].at[d - 1],
            send_sem.at[stage, k, d - 1], recv_sem.at[stage, k, d - 1],
            device_id=device_at(moved(here, axis, d)), device_id_type=mesh,
        )

    turns = (2, 1, 3, 0)
    for d in turns:
        for k in range(3):
            swap(k, d).start()
            load(k, d).start()
    for d in turns:
        for k in range(3):
            load(k, d).wait()
            swap(k, d).wait_recv()
            q = (here[ORDERS[k][0]] + d) % 4

            @pl.loop(0, 32)
            def _(n):
                own[k][q, n] = own[k][q, n] + pair[k][q, n]

            if d:
                pass_on(0, k, d).start()

    def total(stage, k, n):
        mine = sources[stage][k][here[ORDERS[k][stage]], n].astype(jnp.float32)
        for d in range(3):
            mine = mine + lands[stage][k][d, n].astype(jnp.float32)
        return mine.astype(jnp.bfloat16)

    for stage in (0, 1):
        later = sources[stage + 1]
        count = 8 if stage == 0 else 2
        for k in range(3):
            for d in (1, 2, 3):
                pass_on(stage, k, d).wait_recv()

            @pl.loop(0, 4)
            def _(q):
                for n in range(count):
                    later[k][q, n] = total(stage, k, q * count + n)

            for d in (2, 1, 3):
                pass_on(stage + 1, k, d).start()

    col = here["z"] * 2 + here["x"] // 2
    own_rows = pl.multiple_of(here["core"] * SIZE, SIZE)
    for k in range(3):
        for d in (1, 2, 3):
            pass_on(2, k, d).wait_recv()
        for b in range(2):
            row_buf[pl.ds(own_rows + STARTS[k], SHARES[k]), pl.ds(pl.multiple_of(col * 256 + b * SIZE, SIZE), SIZE)] = total(2, k, b)

    def tile(spot):
        c = spot["z"] * 2 + spot["x"] // 2
        return row_buf.at[pl.ds(own_rows, SIZE), pl.ds(pl.multiple_of(c * 256, 256), 256)]

    def spread(dz, dx):
        return pltpu.make_async_remote_copy(
            tile(here), tile(here), gather_send.at[dz * 2 + dx], gather_recv.at[dz * 2 + dx],
            device_id=device_at(moved(moved(here, "x", 2 * dx), "z", dz)), device_id_type=mesh,
        )

    def share(dz, dx):
        spot = moved(moved(here, "x", 2 * dx), "z", -dz)
        return pltpu.make_async_remote_copy(
            tile(spot), tile(spot), share_send.at[dz * 2 + dx], share_recv.at[dz * 2 + dx],
            device_id=device_at(partner), device_id_type=mesh,
        )

    steps = ((2, 1), (1, 1), (3, 1), (2, 0), (0, 1), (1, 0), (3, 0))
    for step in steps:
        spread(*step).start()
    share(0, 0).start()
    for step in steps[::-1]:
        spread(*step).wait_recv()
        share(*step).start()
    for step in ((0, 0),) + steps:
        share(*step).wait()
    for step in steps:
        spread(*step).wait_send()
    done = pltpu.make_async_copy(row_buf, out_ref, out_sem)
    done.start()
    for k in range(3):
        for d in turns:
            swap(k, d).wait_send()
        for stage in range(3):
            for d in (1, 2, 3):
                pass_on(stage, k, d).wait_send()
    done.wait()


def reduced_row(parts):
    def buffers(*lead):
        return [pltpu.VMEM((*lead, share, SIZE), jnp.bfloat16) for share in SHARES]

    dma = pltpu.SemaphoreType.DMA
    hbm = pl.BlockSpec(memory_space=pl.ANY)
    return pl.pallas_call(
        reduce_kernel,
        out_shape=jax.ShapeDtypeStruct((2 * SIZE, 16 * SIZE), jnp.bfloat16),
        in_specs=[hbm] * 3,
        out_specs=hbm,
        scratch_shapes=[
            *buffers(4, 32), *buffers(4, 32),
            *buffers(3, 32), *buffers(4, 8),
            *buffers(3, 8), *buffers(4, 2),
            *buffers(3, 2),
            pltpu.VMEM((2 * SIZE, 16 * SIZE), jnp.bfloat16),
            dma((3, 4)), dma((3, 4)), dma((3, 4)), dma((3, 3, 3)), dma((3, 3, 3)),
            dma((8,)), dma((8,)), dma((8,)), dma((8,)), dma,
        ],
        compiler_params=pltpu.CompilerParams(
            collective_id=0, has_side_effects=True, vmem_limit_bytes=58 << 20
        ),
        cost_estimate=pl.CostEstimate(flops=1 << 33, bytes_accessed=64 << 20, transcendentals=0),
    )(*parts)


def local(
    basis_values,
    potential,
    pair_atoms,
    target_device,
    target_block,
    density,
    density_mask,
    inverse_intersection,
    inverse_mask,
):
    atoms, _, size = basis_values.shape
    tile_blocks = density_mask.shape[0]
    devices = lax.axis_size(ALL)
    per_owner = tile_blocks * tile_blocks // lax.axis_size("panel")
    empty = atoms * atoms

    target = target_device[:, 0] * per_owner + target_block
    serial = jnp.arange(target.shape[0], dtype=jnp.int32)
    key = serial * empty + pair_atoms[0] * atoms + pair_atoms[1]
    hit = target[None, :] == jnp.arange(devices * per_owner, dtype=jnp.int32)[:, None]
    low = jnp.min(jnp.where(hit, key[None, :], 1 << 30), axis=1)
    high = jnp.max(jnp.where(hit, key[None, :], -1), axis=1)
    first = jnp.where(high >= 0, low % empty, empty)
    second = jnp.where(high > low, high % empty, empty)

    density_used = masked_blocks(density, density_mask, size)
    inverse_used = masked_blocks(inverse_intersection, inverse_mask, size)
    width = inverse_used.shape[1] // lax.axis_size("panel")
    own = lax.dynamic_slice_in_dim(inverse_used, lax.axis_index("panel") * width, width, 1)
    density_used, own, first = lax.optimization_barrier((density_used, own, first))
    p_rows = lax.all_gather(density_used, "col", axis=1, tiled=True)
    s_cols = lax.all_gather(own, "row", axis=0, tiled=True)
    parts = gram_blocks(first, second, potential, basis_values)
    product = jnp.dot(p_rows, s_cols, preferred_element_type=jnp.float32).astype(jnp.bfloat16)
    product, *parts = lax.optimization_barrier((product, *parts))
    x_cols = lax.all_gather(product, "row", axis=0, tiled=True)
    hamiltonian = reduced_row(parts)
    return jnp.dot(hamiltonian, x_cols, preferred_element_type=jnp.float32)


def solution(mesh):
    placed = (
        P(ALL, None, None),
        P(ALL),
        P(None, ALL),
        P(ALL, None),
        P(ALL),
        P("row", "col"),
        P("row", "col"),
        P("row", "col"),
        P("row", "col"),
    )
    return jax.shard_map(
        local, mesh=mesh, in_specs=placed, out_specs=P("row", ("col", "panel")), check_vma=False
    )
```

time: 508 us -> 178 us (0.35)
  local copies, waits for them, and re-layouts: 158 us -> 0.32 us
  Pallas kernels: 0 us -> 127 us
  waiting for transfers between devices: 132 us -> 25.6 us
  starting transfers between devices: 95 us -> 0.08 us
  matrix products: 82.6 us -> 5.32 us
  blocking collectives: 22.3 us -> 0 us
  between operations: 0.31 us -> 13.2 us
  other arithmetic: 16.2 us -> 5.29 us
    gather x16 -> x0, local copies, waits for them, and re-layouts: 130 us -> none  [the longest x8 64.9 us: one_group(): left_rows = basis_values[pair_ids[0]]]
    pallas_call x0 -> x2, Pallas kernels: none -> 127 us  [the longest x1 68.8 us: reduced_row(): pl.pallas_call(reduce_kernel, out_shape=jax.ShapeDtypeStruct((2 * SIZE, 1...]
    all_to_all x2 -> x0, waiting for transfers between devices: 94.4 us -> none  [the longest x1 94.4 us: local(): lax.all_to_all(outgoing, ('row', 'col', 'panel'), split_axis=0, concat_ax...]
    ppermute x24 -> x0, starting transfers between devices: 80.6 us -> none  [shifted_2(): return lax.ppermute(block, axis, route)]
    dot_general x17 -> x2, matrix products: 82.6 us -> 5.32 us  [the longest x1 2.68 us: local(): return jnp.dot(hamiltonian, x_cols, preferred_element_type=jnp.float32)]
    ppermute x24 -> x0, waiting for transfers between devices: 37.3 us -> none  [shifted_2(): return lax.ppermute(block, axis, route)]
    all_gather x0 -> x3, waiting for transfers between devices: none -> 24.9 us  [the longest x1 24.9 us: local(): s_cols = lax.all_gather(own, 'row', axis=0, tiled=True)]
    scatter x2 -> x0, local copies, waits for them, and re-layouts: 20.7 us -> none  [the longest x1 19.6 us: local(): outgoing = jnp.zeros((devices * capacity, block_size, block_size), jnp.bf...]
  transfers between devices with their start and end apart: 26 -> 3, of which waited for: 12 -> 1; matrix products, arithmetic and copies ran while one was open for 50% -> 0% of each run, Pallas kernels for 0% -> 72%
where the time goes in v1:
time: 178 us; the launch traced here: 177 us
  Pallas kernels  127 us (71%)
  waiting for transfers between devices  25.6 us (14%)
  between operations  13.2 us (7%)
  matrix products  5.32 us (3%)
  other arithmetic  5.29 us (3%)
    pallas_call x1, Pallas kernels, reduced_row(): pl.pallas_call(reduce_kernel, out_shape=jax.ShapeDtypeStruct((2 * SIZE, 1...  68.8 us
    pallas_call x1, Pallas kernels, gram_blocks(): pl.pallas_call(gram_kernel, out_shape=[jax.ShapeDtypeStruct((2, 4, 32, sh...  58.7 us
    all_gather x1, waiting for transfers between devices, local(): s_cols = lax.all_gather(own, 'row', axis=0, tiled=True)  24.9 us
  transfers between devices with their start and end apart: 3, of which 1 were waited for; matrix products, arithmetic and copies ran while one was open for 0% of the time, Pallas kernels for 72%

profile of v1, /device:TPU:1, one launch (start us, length us, event | category | flops | bytes accessed | tf_op | source)
XLA Modules:
  0.0 177.3 jit_solution(310591863583630111)
XLA Ops:
  6.5 0.0 all-gather.4.cloned.1.call-start
  6.5 0.8 add_bitcast_fusion
  7.3 0.7 convert_element_type.9
  8.0 0.7 convert_element_type.10
  8.7 0.1 mul.57
  8.9 0.7 bitcast_add_fusion
  9.5 0.1 select_reduce_fusion
  9.7 0.6 compare_select_fusion.4
  10.3 0.1 mul.54
  10.4 1.7 bitcast_multiply_fusion
  12.2 0.0 all-gather.4.cloned.1.call-update
  12.2 0.0 all-gather.6.cloned.1.call-start
  12.2 0.7 all-gather.6.cloned.1.call-update
  12.9 0.0 all-gather.8.cloned.1.call-start
  13.0 58.7 %shard_map.91 = (bf16[2,4,32,48,128]{4,3,2,1,0:T(8,128)(2,1)}, bf16[2,4,32,48,128]{4,3,2,1,0:T(8,128)(2,1)}, bf16[2,4,32,32,128]{4,3,2,1,0:T(8,128)(2,1)}) custom-call(s32[256]{0:T(256)} %get-tuple-element.17.first_ref, s32[256]{0:T(256)} %get-tuple-element.27.second_ref, f32[16,128]{1,0:T(8,128)} %bitcast.21, bf16[16,2048,128]{2,1,0:T(8,128)(2,1)} %basis_ref.1), custom_call_target="tpu_custom_call" | custom-call | flops 17179869184 | bytes 20971520 | tf_op jit(solution)/shard_map/pallas_call | solution.py:77
  71.7 0.0 all-gather.4.cloned.1.call-done
  71.7 24.9 %all-gather.6.cloned.1.call-done = bf16[2048,256]{1,0:T(8,128)(2,1)} async-done(((bf16[256,256]{1,0:T(8,128)(2,1)}), bf16[2048,256]{1,0:T(8,128)(2,1)}) %all-gather.6.cloned.1.call-update) | async-done | bytes 1048592 | tf_op jit(solution)/shard_map/all_gather | solution.py:298
  96.6 2.6 %convolution_convert_fusion = bf16[256,256]{1,0:T(8,128)(2,1)} fusion(bf16[256,2048]{1,0:T(8,128)(2,1)} %all-gather.4.cloned.1.call-done, bf16[2048,256]{1,0:T(8,128)(2,1)} %all-gather.6.cloned.1.call-done), kind=kOutput, calls=%fused_computation | convolution fusion | flops 268500992 | bytes 2228224 | tf_op jit(solution)/shard_map/dot_general | solution.py:300
  99.2 0.0 all-gather.8.cloned.1.call-update
  99.2 68.8 %shard_map.92 = bf16[256,2048]{1,0:T(8,128)(2,1)} custom-call(bf16[2,4,32,48,128]{4,3,2,1,0:T(8,128)(2,1)} %get-tuple-element.21.in0, bf16[2,4,32,48,128]{4,3,2,1,0:T(8,128)(2,1)} %get-tuple-element.22.in1, bf16[2,4,32,32,128]{4,3,2,1,0:T(8,128)(2,1)} %get-tuple-element.23.in2), custom_call_target="tpu_custom_call" | custom-call | flops 8589934592 | bytes 67108864 | tf_op jit(solution)/shard_map/pallas_call | solution.py:245
  168.0 0.0 all-gather.8.cloned.1.call-done
  168.1 2.7 %fusion.2 = f32[256,256]{1,0:T(8,128)} fusion(bf16[256,2048]{1,0:T(8,128)(2,1)} %shard_map.92, bf16[2048,256]{1,0:T(8,128)(2,1)} %all-gather.8.cloned.1.call-done), kind=kOutput, calls=%fused_computation.19 | convolution fusion | flops 268435456 | bytes 2359296 | tf_op jit(solution)/shard_map/dot_general | solution.py:304
  (1 shorter events, 0.0 us)
Async XLA Ops:
  6.5 65.1 %all-gather.4.cloned.1.call-start = ((), (), s32[]{:S(2)}) async-start(), calls=%async_computation | async-start | bytes 1179648 | tf_op jit(solution)/shard_map/all_gather | solution.py:297
  12.2 84.4 %all-gather.6.cloned.1.call-start = ((), (), s32[]{:S(2)}) async-start(), calls=%async_computation.1 | async-start | bytes 1179648 | tf_op jit(solution)/shard_map/all_gather | solution.py:298
  12.9 155.1 %all-gather.8.cloned.1.call-start = ((), (), s32[]{:S(2)}) async-start(), calls=%async_computation.2 | async-start | bytes 1179648 | tf_op jit(solution)/shard_map/all_gather | solution.py:302
Sparse Core Ops, SparseCore 0:
  12.3 47.8 all-gather.3
  61.8 34.6 all-gather.5
  99.3 52.5 all-gather.7

commit v2 on v1

v2 whole, which is shorter than its diff:
```python
import functools

import jax
import jax.numpy as jnp
from jax import lax
from jax.experimental import pallas as pl
from jax.experimental.pallas import tpu as pltpu
from jax.sharding import PartitionSpec as P

ALL = ("row", "col", "panel")


def masked_blocks(matrix, block_mask, block_size):
    mask_rows, mask_cols = block_mask.shape
    shaped = matrix.reshape(mask_rows, block_size, mask_cols, block_size)
    factor = block_mask.astype(matrix.dtype)[:, None, :, None]
    return (shaped * factor).reshape(mask_rows * block_size, mask_cols * block_size)


SIZE = 128
SHARES = (48, 48, 32)
STARTS = (0, 48, 96)
ORDERS = (("x", "y", "z"), ("y", "z", "x"), ("z", "x", "y"))


def place():
    row, col, core = (lax.axis_index(axis) for axis in ALL)
    return {"x": col % 2 * 2 + row % 2, "y": row // 2, "z": col // 2, "core": core}


def device_at(spot):
    return (spot["y"] * 2 + spot["x"] % 2, spot["z"] * 2 + spot["x"] // 2, spot["core"])


def moved(spot, axis, steps):
    return {**spot, axis: (spot[axis] + steps) % (2 if axis == "core" else 4)}


def tile_column(spot):
    return spot["z"] * 2 + spot["x"] // 2


def tile_row(spot):
    return spot["y"] * 2 + spot["x"] % 2


def in_row(spot, dz, dx):
    return moved(moved(spot, "x", 2 * dx), "z", dz)


def in_column(spot, dy, dx):
    return moved({**spot, "x": spot["x"] // 2 * 2 + (spot["x"] + dx) % 2}, "y", dy)


STEPS = ((2, 1), (1, 1), (3, 1), (2, 0), (0, 1), (1, 0), (3, 0))


def whole_kernel(
    first_ref, second_ref, weight_ref, basis_ref, density_ref, inverse_ref, out_ref,
    raw, left, right, blocks, column,
    own0, own1, own2, give0, give1, give2, pair0, pair1, pair2,
    relay0, relay1, relay2, near0, near1, near2, one0, one1, one2,
    got20, got21, got22, two0, two1, two2, got30, got31, got32,
    p_row, s_col, x_col, row_buf,
    fetch_sem, pair_send, pair_recv, relay_send, relay_recv, near_send, near_recv, send_sem, recv_sem,
    p_send, p_recv, s_send, s_recv, x_send, x_recv, gather_send, gather_recv, share_send, share_recv,
):
    here = place()
    own, give, pair = (own0, own1, own2), (give0, give1, give2), (pair0, pair1, pair2)
    relay, near, one = (relay0, relay1, relay2), (near0, near1, near2), (one0, one1, one2)
    two = (two0, two1, two2)
    sources, lands = (None, one, two), (None, (got20, got21, got22), (got30, got31, got32))
    partner = moved(here, "core", 1)
    mesh = pl.DeviceIdType.MESH
    atoms, points, size = basis_ref.shape
    chunks = points // size
    slots = raw.shape[0]

    def fetch(a):
        return pltpu.make_async_copy(basis_ref.at[a], raw.at[a % slots], fetch_sem.at[a])

    for a in range(slots):
        fetch(a).start()

    peers = [partner]
    for axis in ("x", "y", "z"):
        peers += [moved(here, axis, d) for d in (1, 2, 3)]
    peers += [in_row(here, d, 1) for d in (1, 2, 3)]
    peers += [in_column(here, d, 1) for d in (1, 2, 3)]
    barrier = pltpu.get_barrier_semaphore()
    for peer in peers:
        pl.semaphore_signal(barrier, inc=1, device_id=device_at(peer), device_id_type=mesh)

    for k in range(chunks):
        spread_row = jnp.broadcast_to(weight_ref[k : k + 1, :], (size, size))
        column[k * size : (k + 1) * size, :] = spread_row.T
    blocks[atoms * atoms] = jnp.zeros((size, size), jnp.bfloat16)

    def remote(src, dst, send, recv, spot):
        return pltpu.make_async_remote_copy(
            src_ref=src, dst_ref=dst, send_sem=send, recv_sem=recv,
            device_id=device_at(spot), device_id_type=mesh,
        )

    tile = 2 * size
    own_col = pl.ds(pl.multiple_of(tile_column(here) * tile, tile), tile)
    own_row = pl.ds(pl.multiple_of(tile_row(here) * tile, tile), tile)

    def send_p(dz, dx):
        at = dz * 2 + dx
        return remote(density_ref, p_row.at[:, own_col], p_send.at[at], p_recv.at[at], in_row(here, dz, dx))

    def send_s(dy, dx):
        at = dy * 2 + dx
        return remote(inverse_ref, s_col.at[own_row, :], s_send.at[at], s_recv.at[at], in_column(here, dy, dx))

    def send_x(dy, dx):
        at = dy * 2 + dx
        rows = x_col.at[own_row, :]
        return remote(rows, rows, x_send.at[at], x_recv.at[at], in_column(here, dy, dx))

    pl.semaphore_wait(barrier, len(peers))
    for step in STEPS:
        send_p(*step).start()
        send_s(*step).start()
    p_row[:, own_col] = density_ref[...]
    s_col[own_row, :] = inverse_ref[...]

    @pl.loop(0, atoms)
    def _(a):
        fetch(a).wait()
        cols = pl.ds(pl.multiple_of(a * size, size), size)
        for k in range(chunks):
            rows = pl.ds(k * size, size)
            piece = raw[a % slots, rows, :]
            left[cols, rows] = piece.T
            scaled = piece.astype(jnp.float32) * column[rows, :]
            right[rows, cols] = scaled.astype(jnp.bfloat16)

        @pl.when(a < atoms - slots)
        def _():
            fetch(a + slots).start()

    @pl.loop(0, atoms // 2)
    def _(j):
        cols = pl.ds(pl.multiple_of(j * 2 * size, 2 * size), 2 * size)
        product = jnp.dot(left[...], right[:, cols], preferred_element_type=jnp.float32)
        for u in range(atoms):
            for v in range(2):
                part = product[u * size : (u + 1) * size, v * size : (v + 1) * size]
                blocks[u * atoms + j * 2 + v] = part.astype(jnp.bfloat16)

    for step in STEPS:
        send_p(*step).wait_recv()
        send_s(*step).wait_recv()
    x_col[own_row, :] = jnp.dot(p_row[...], s_col[...], preferred_element_type=jnp.float32).astype(jnp.bfloat16)
    for step in STEPS:
        send_x(*step).start()

    def spot_of(k, d):
        return (here[ORDERS[k][0]] + d) % 4

    def assembled(k, q, m, g, core):
        at = dict(zip(ORDERS[k], (q, m, g // 2)))
        n = ((tile_row(at) * 8 + tile_column(at)) * 2 + core) * 2 + g % 2
        rows = pl.ds(STARTS[k], SHARES[k])
        return blocks[first_ref[n], rows, :] + blocks[second_ref[n], rows, :]

    def swap(k, d):
        q = spot_of(k, d)
        return remote(give[k].at[q], pair[k].at[q], pair_send.at[k, d], pair_recv.at[k, d], partner)

    def pass_relay(k, side):
        half = pl.ds(16 * side, 16)
        return remote(
            own[k].at[spot_of(k, 2), half], relay[k].at[side], relay_send.at[k, side], relay_recv.at[k, side],
            moved(here, ORDERS[k][0], 3 if side else 1),
        )

    def pass_near(k, side, part):
        half = pl.ds(16 * part, 16)
        d = 3 if side else 1
        return remote(
            own[k].at[spot_of(k, d), half], near[k].at[side, half],
            near_send.at[k, side, part], near_recv.at[k, side, part], moved(here, ORDERS[k][0], d),
        )

    def pass_on(stage, k, d):
        axis = ORDERS[k][stage]
        return remote(
            sources[stage][k].at[(here[axis] + d) % 4], lands[stage][k].at[d - 1],
            send_sem.at[stage - 1, k, d - 1], recv_sem.at[stage - 1, k, d - 1], moved(here, axis, d),
        )

    turns = (2, 1, 3, 0)
    for d in turns:
        for k in range(3):
            q = spot_of(k, d)

            @pl.loop(0, 4)
            def _(m):
                for g in range(8):
                    give[k][q, m * 8 + g] = assembled(k, q, m, g, partner["core"])

            swap(k, d).start()
    for d in turns:
        for k in range(3):
            q = spot_of(k, d)
            swap(k, d).wait_recv()

            @pl.loop(0, 4)
            def _(m):
                for g in range(8):
                    own[k][q, m * 8 + g] = assembled(k, q, m, g, here["core"]) + pair[k][q, m * 8 + g]

            if d == 2:
                pass_relay(k, 0).start()
                pass_relay(k, 1).start()
            if d == 1:
                pass_near(k, 0, 1).start()
            if d == 3:
                pass_near(k, 1, 0).start()
    for k in range(3):
        for side in range(2):
            q = spot_of(k, 3 if side else 1)
            pass_relay(k, side).wait_recv()

            @pl.loop(0, 4)
            def _(m):
                for g in range(4):
                    n = m * 4 + g
                    own[k][q, 16 * side + n] = own[k][q, 16 * side + n] + relay[k][side, n]

            pass_near(k, side, side).start()
    for k in range(3):
        q = spot_of(k, 0)
        for side in range(2):
            for part in range(2):
                pass_near(k, side, part).wait_recv()

        @pl.loop(0, 4)
        def _(m):
            for g in range(8):
                n = m * 8 + g
                total = own[k][q, n].astype(jnp.float32) + near[k][0, n].astype(jnp.float32)
                one[k][m, g] = (total + near[k][1, n].astype(jnp.float32)).astype(jnp.bfloat16)

        for d in (2, 1, 3):
            pass_on(1, k, d).start()

    def added(stage, k, n):
        mine = sources[stage][k][here[ORDERS[k][stage]], n].astype(jnp.float32)
        for d in range(3):
            mine = mine + lands[stage][k][d, n].astype(jnp.float32)
        return mine.astype(jnp.bfloat16)

    for k in range(3):
        for d in (1, 2, 3):
            pass_on(1, k, d).wait_recv()
        for q in range(4):
            for b in range(2):
                two[k][q, b] = added(1, k, q * 2 + b)
        for d in (2, 1, 3):
            pass_on(2, k, d).start()

    core_row = pl.multiple_of(here["core"] * size, size)
    for k in range(3):
        for d in (1, 2, 3):
            pass_on(2, k, d).wait_recv()
        for b in range(2):
            cols = pl.ds(pl.multiple_of(tile_column(here) * tile + b * size, size), size)
            row_buf[pl.ds(core_row + STARTS[k], SHARES[k]), cols] = added(2, k, b)

    def tile_of(spot):
        cols = pl.ds(pl.multiple_of(tile_column(spot) * tile, tile), tile)
        return row_buf.at[pl.ds(core_row, size), cols]

    def spread(dz, dx):
        at = dz * 2 + dx
        return remote(tile_of(here), tile_of(here), gather_send.at[at], gather_recv.at[at], in_row(here, dz, dx))

    def share(dz, dx):
        at = dz * 2 + dx
        from_there = tile_of(in_row(here, 4 - dz, dx))
        return remote(from_there, from_there, share_send.at[at], share_recv.at[at], partner)

    for step in STEPS:
        spread(*step).start()
    share(0, 0).start()
    for step in STEPS:
        send_x(*step).wait_recv()
    for step in STEPS[::-1]:
        spread(*step).wait_recv()
        share(*step).start()
    for step in ((0, 0),) + STEPS:
        share(*step).wait_recv()
    out_ref[...] = jnp.dot(row_buf[...], x_col[...], preferred_element_type=jnp.float32)

    for step in STEPS:
        for copy in (send_p, send_s, send_x, spread, share):
            copy(*step).wait_send()
    share(0, 0).wait_send()
    for k in range(3):
        for d in turns:
            swap(k, d).wait_send()
        for side in range(2):
            pass_relay(k, side).wait_send()
            for part in range(2):
                pass_near(k, side, part).wait_send()
        for stage in (1, 2):
            for d in (1, 2, 3):
                pass_on(stage, k, d).wait_send()


def gradient_tile(first, second, weights, basis, density, inverse):
    atoms, points, size = basis.shape
    depth = 16 * size

    def buffers(*lead):
        return [pltpu.VMEM((*lead, share, size), jnp.bfloat16) for share in SHARES]

    def plain(*shape):
        return pltpu.VMEM(shape, jnp.bfloat16)

    dma = pltpu.SemaphoreType.DMA
    vmem = pl.BlockSpec(memory_space=pltpu.VMEM)
    smem = pl.BlockSpec(memory_space=pltpu.SMEM)
    return pl.pallas_call(
        whole_kernel,
        out_shape=jax.ShapeDtypeStruct((2 * size, 2 * size), jnp.float32),
        in_specs=[smem, smem, vmem, pl.BlockSpec(memory_space=pl.ANY), vmem, vmem],
        out_specs=vmem,
        scratch_shapes=[
            plain(atoms // 2, points, size), plain(atoms * size, points), plain(points, atoms * size),
            plain(atoms * atoms + 1, size, size), pltpu.VMEM((points, size), jnp.float32),
            *buffers(4, 32), *buffers(4, 32), *buffers(4, 32),
            *buffers(2, 16), *buffers(2, 32), *buffers(4, 8),
            *buffers(3, 8), *buffers(4, 2), *buffers(3, 2),
            plain(2 * size, depth), plain(depth, 2 * size), plain(depth, 2 * size), plain(2 * size, depth),
            dma((atoms,)), dma((3, 4)), dma((3, 4)), dma((3, 2)), dma((3, 2)), dma((3, 2, 2)), dma((3, 2, 2)),
            dma((2, 3, 3)), dma((2, 3, 3)),
            *[dma((8,)) for _ in range(10)],
        ],
        compiler_params=pltpu.CompilerParams(
            collective_id=0, has_side_effects=True, vmem_limit_bytes=60 << 20
        ),
        cost_estimate=pl.CostEstimate(
            flops=2 * (atoms * size) ** 2 * points, bytes_accessed=20 << 20, transcendentals=0
        ),
    )(first, second, weights.reshape(-1, size), basis, density, inverse)


def local(
    basis_values,
    potential,
    pair_atoms,
    target_device,
    target_block,
    density,
    density_mask,
    inverse_intersection,
    inverse_mask,
):
    atoms, _, size = basis_values.shape
    tile_blocks = density_mask.shape[0]
    devices = lax.axis_size(ALL)
    per_owner = tile_blocks * tile_blocks // lax.axis_size("panel")
    empty = atoms * atoms

    target = target_device[:, 0] * per_owner + target_block
    serial = jnp.arange(target.shape[0], dtype=jnp.int32)
    key = serial * empty + pair_atoms[0] * atoms + pair_atoms[1]
    hit = target[None, :] == jnp.arange(devices * per_owner, dtype=jnp.int32)[:, None]
    low = jnp.min(jnp.where(hit, key[None, :], 1 << 30), axis=1)
    high = jnp.max(jnp.where(hit, key[None, :], -1), axis=1)
    first = jnp.where(high >= 0, low % empty, empty)
    second = jnp.where(high > low, high % empty, empty)

    density_used = masked_blocks(density, density_mask, size)
    inverse_used = masked_blocks(inverse_intersection, inverse_mask, size)
    width = inverse_used.shape[1] // lax.axis_size("panel")
    own = lax.dynamic_slice_in_dim(inverse_used, lax.axis_index("panel") * width, width, 1)
    return gradient_tile(first, second, potential, basis_values, density_used, own)


def solution(mesh):
    placed = (
        P(ALL, None, None),
        P(ALL),
        P(None, ALL),
        P(ALL, None),
        P(ALL),
        P("row", "col"),
        P("row", "col"),
        P("row", "col"),
        P("row", "col"),
    )
    return jax.shard_map(
        local, mesh=mesh, in_specs=placed, out_specs=P("row", ("col", "panel")), check_vma=False
    )
```

time: 178 us -> 89.5 us (0.50)
  Pallas kernels: 127 us -> 81.9 us
  waiting for transfers between devices: 25.6 us -> 0 us
  between operations: 13.2 us -> 0.03 us
  matrix products: 5.32 us -> 0 us
    pallas_call x2 -> x1, Pallas kernels: 127 us -> 81.9 us  [gradient_tile(): pl.pallas_call(whole_kernel, out_shape=jax.ShapeDtypeStruct((2 * size, 2...]
    all_gather x3 -> x0, waiting for transfers between devices: 24.9 us -> none  [the longest x1 24.9 us: local(): s_cols = lax.all_gather(own, 'row', axis=0, tiled=True)]
    dot_general x2 -> x0, matrix products: 5.32 us -> none  [the longest x1 2.68 us: local(): return jnp.dot(hamiltonian, x_cols, preferred_element_type=jnp.float32)]
  transfers between devices with their start and end apart: 3 -> 0, of which waited for: 1 -> 0; matrix products, arithmetic and copies ran while one was open for 0% -> 0% of each run, Pallas kernels for 72% -> 0%
where the time goes in v2:
time: 89.5 us; the launch traced here: 89.2 us
  Pallas kernels  81.9 us (92%)
  other arithmetic  5.29 us (6%)
  local copies, waits for them, and re-layouts  1.99 us (2%)
    pallas_call x1, Pallas kernels, gradient_tile(): pl.pallas_call(whole_kernel, out_shape=jax.ShapeDtypeStruct((2 * size, 2...  81.9 us

profile of v2, /device:TPU:1, one launch (start us, length us, event | category | flops | bytes accessed | tf_op | source)
XLA Modules:
  0.0 89.2 jit_solution(9373873647003061598)
XLA Ops:
  0.0 0.7 convert_element_type.7
  0.7 0.1 mul.64
  0.9 0.7 convert_element_type.6
  1.6 0.1 mul.61
  1.7 1.7 %bitcast_multiply_fusion = (bf16[256,256]{1,0:T(8,128)(2,1)}, bf16[256,256]{1,0:T(8,128)(2,1)}) fusion(bf16[256,256]{1,0:T(8,128)(2,1)} %param.14, bf16[32,8,2,128]{3,2,1,0:T(2,128)(2,1)S(1)} %bitcast.16, bf16[256,512]{1,0:T(8,128)(2,1)S(1)} %bitcast.15, s32[]{:T(128)S(6)} %select_n.34, bf16[256,512]{1,0:T(8,128)(2,1)} %param.16), kind=kLoop, calls=%fused_computation.1 | loop fusion | flops 524288 | bytes 786436 | tf_op jit(solution)/shard_map/mul | solution.py:17
  3.5 0.8 add_bitcast_fusion
  4.2 0.7 bitcast_add_fusion
  4.9 0.1 select_reduce_fusion
  5.0 0.6 compare_select_fusion.4
  5.6 81.9 %shard_map.91 = f32[256,256]{1,0:T(8,128)} custom-call(s32[256]{0:T(256)} %get-tuple-element.8.first_ref, s32[256]{0:T(256)} %get-tuple-element.7.second_ref, f32[16,128]{1,0:T(8,128)} %bitcast.17, bf16[16,2048,128]{2,1,0:T(8,128)(2,1)} %basis_ref.1, bf16[256,256]{1,0:T(8,128)(2,1)} %get-tuple-element.9.density_ref, ...), custom_call_target="tpu_custom_call" | custom-call | flops 17179869184 | bytes 20971520 | tf_op jit(solution)/shard_map/pallas_call | solution.py:328
  87.6 1.7 %copy.16 = f32[256,256]{1,0:T(8,128)} copy(f32[256,256]{1,0:T(8,128)} %shard_map.91) | data formatting | bytes 524288
  (1 shorter events, 0.0 us)

commit v3 on v2

--- a/solution.py
+++ b/solution.py
@@ -20,7 +20,7 @@
 SIZE = 128
 SHARES = (48, 48, 32)
 STARTS = (0, 48, 96)
-ORDERS = (("x", "y", "z"), ("y", "z", "x"), ("z", "x", "y"))
+ORDERS = (("x", "y", "z"), ("z", "x", "y"), ("y", "z", "x"))
 
 
 def place():
@@ -44,15 +44,68 @@
     return spot["y"] * 2 + spot["x"] % 2
 
 
-def in_row(spot, dz, dx):
-    return moved(moved(spot, "x", 2 * dx), "z", dz)
-
-
-def in_column(spot, dy, dx):
-    return moved({**spot, "x": spot["x"] // 2 * 2 + (spot["x"] + dx) % 2}, "y", dy)
-
-
 STEPS = ((2, 1), (1, 1), (3, 1), (2, 0), (0, 1), (1, 0), (3, 0))
+
+
+class Gather:
+    def __init__(self, here, ring, mirror, view, send, recv):
+        self.here, self.ring, self.mirror, self.view, self.send, self.recv = here, ring, mirror, view, send, recv
+
+    def spot(self, steps, image):
+        there = moved(self.here, self.ring, steps)
+        x = there["x"]
+        if image and self.mirror == "x_hi":
+            x = (x + 2) % 4
+        elif image:
+            x = x // 2 * 2 + (x + 1) % 2
+        return {**there, "x": x}
+
+    def copy(self, ref, at, spot):
+        return pltpu.make_async_remote_copy(
+            src_ref=ref, dst_ref=ref, send_sem=self.send.at[at], recv_sem=self.recv.at[at],
+            device_id=device_at(spot), device_id_type=pl.DeviceIdType.MESH,
+        )
+
+    def cross(self):
+        return self.copy(self.view(self.here, None), 0, self.spot(0, 1))
+
+    def hop(self, side, image):
+        ref = self.view(self.spot(0, image), None)
+        return self.copy(ref, 1 + side * 2 + image, self.spot(3 if side else 1, 0))
+
+    def far(self, side, image):
+        ref = self.view(self.spot(1 if side else 3, image), side)
+        return self.copy(ref, 5 + side * 2 + image, self.spot(3 if side else 1, 0))
+
+    def begin(self):
+        self.cross().start()
+        self.hop(0, 0).start()
+        self.hop(1, 0).start()
+
+    def second(self):
+        self.cross().wait_recv()
+        for side in range(2):
+            self.hop(side, 1).start()
+        for side in range(2):
+            self.hop(side, 0).wait_recv()
+            self.far(side, 0).start()
+
+    def third(self):
+        for side in range(2):
+            self.hop(side, 1).wait_recv()
+            self.far(side, 1).start()
+
+    def finish(self):
+        for side in range(2):
+            for image in range(2):
+                self.far(side, image).wait_recv()
+
+    def sent(self):
+        self.cross().wait_send()
+        for side in range(2):
+            for image in range(2):
+                self.hop(side, image).wait_send()
+                self.far(side, image).wait_send()
 
 
 def whole_kernel(
@@ -85,8 +138,7 @@
     peers = [partner]
     for axis in ("x", "y", "z"):
         peers += [moved(here, axis, d) for d in (1, 2, 3)]
-    peers += [in_row(here, d, 1) for d in (1, 2, 3)]
-    peers += [in_column(here, d, 1) for d in (1, 2, 3)]
+    peers += [moved(moved(here, "x", 2), "z", d) for d in (1, 2, 3)]
     barrier = pltpu.get_barrier_semaphore()
     for peer in peers:
         pl.semaphore_signal(barrier, inc=1, device_id=device_at(peer), device_id_type=mesh)
@@ -106,56 +158,56 @@
     own_col = pl.ds(pl.multiple_of(tile_column(here) * tile, tile), tile)
     own_row = pl.ds(pl.multiple_of(tile_row(here) * tile, tile), tile)
 
-    def send_p(dz, dx):
-        at = dz * 2 + dx
-        return remote(density_ref, p_row.at[:, own_col], p_send.at[at], p_recv.at[at], in_row(here, dz, dx))
-
-    def send_s(dy, dx):
-        at = dy * 2 + dx
-        return remote(inverse_ref, s_col.at[own_row, :], s_send.at[at], s_recv.at[at], in_column(here, dy, dx))
-
-    def send_x(dy, dx):
-        at = dy * 2 + dx
-        rows = x_col.at[own_row, :]
-        return remote(rows, rows, x_send.at[at], x_recv.at[at], in_column(here, dy, dx))
-
-    pl.semaphore_wait(barrier, len(peers))
-    for step in STEPS:
-        send_p(*step).start()
-        send_s(*step).start()
+    def p_view(spot, half):
+        rows = pl.ds(0, tile) if half is None else pl.ds(half * size, size)
+        return p_row.at[rows, pl.ds(pl.multiple_of(tile_column(spot) * tile, tile), tile)]
+
+    def row_view(ref):
+        def view(spot, half):
+            start = tile_row(spot) * tile + (half or 0) * size
+            return ref.at[pl.ds(pl.multiple_of(start, size), tile if half is None else size), :]
+
+        return view
+
+    p_all = Gather(here, "z", "x_hi", p_view, p_send, p_recv)
+    s_all = Gather(here, "y", "x_lo", row_view(s_col), s_send, s_recv)
+    x_all = Gather(here, "y", "x_lo", row_view(x_col), x_send, x_recv)
+
     p_row[:, own_col] = density_ref[...]
     s_col[own_row, :] = inverse_ref[...]
-
-    @pl.loop(0, atoms)
-    def _(a):
+    pl.semaphore_wait(barrier, len(peers))
+    p_all.begin()
+    s_all.begin()
+
+    def prepare(a):
         fetch(a).wait()
-        cols = pl.ds(pl.multiple_of(a * size, size), size)
+        cols = pl.ds(a * size, size)
         for k in range(chunks):
             rows = pl.ds(k * size, size)
             piece = raw[a % slots, rows, :]
             left[cols, rows] = piece.T
             scaled = piece.astype(jnp.float32) * column[rows, :]
             right[rows, cols] = scaled.astype(jnp.bfloat16)
-
-        @pl.when(a < atoms - slots)
-        def _():
+        if a < atoms - slots:
             fetch(a + slots).start()
 
-    @pl.loop(0, atoms // 2)
-    def _(j):
-        cols = pl.ds(pl.multiple_of(j * 2 * size, 2 * size), 2 * size)
-        product = jnp.dot(left[...], right[:, cols], preferred_element_type=jnp.float32)
-        for u in range(atoms):
+    for a in range(atoms):
+        prepare(a)
+    for j in range(0, atoms, 2):
+        cols = pl.ds(j * size, tile)
+        product = jnp.dot(left[: (j + 2) * size, :], right[:, cols], preferred_element_type=jnp.float32)
+        for u in range(j + 2):
             for v in range(2):
-                part = product[u * size : (u + 1) * size, v * size : (v + 1) * size]
-                blocks[u * atoms + j * 2 + v] = part.astype(jnp.bfloat16)
-
-    for step in STEPS:
-        send_p(*step).wait_recv()
-        send_s(*step).wait_recv()
-    x_col[own_row, :] = jnp.dot(p_row[...], s_col[...], preferred_element_type=jnp.float32).astype(jnp.bfloat16)
-    for step in STEPS:
-        send_x(*step).start()
+                part = product[u * size : (u + 1) * size, v * size : (v + 1) * size].astype(jnp.bfloat16)
+                blocks[u * atoms + j + v] = part
+                if u < j:
+                    blocks[(j + v) * atoms + u] = part.T
+        if j == 4:
+            p_all.second()
+            s_all.second()
+        if j == 10:
+            p_all.third()
+            s_all.third()
 
     def spot_of(k, d):
         return (here[ORDERS[k][0]] + d) % 4
@@ -192,8 +244,7 @@
             send_sem.at[stage - 1, k, d - 1], recv_sem.at[stage - 1, k, d - 1], moved(here, axis, d),
         )
 
-    turns = (2, 1, 3, 0)
-    for d in turns:
+    def give_away(d):
         for k in range(3):
             q = spot_of(k, d)
 
@@ -203,7 +254,8 @@
                     give[k][q, m * 8 + g] = assembled(k, q, m, g, partner["core"])
 
             swap(k, d).start()
-    for d in turns:
+
+    def take_in(d):
         for k in range(3):
             q = spot_of(k, d)
             swap(k, d).wait_recv()
@@ -220,8 +272,9 @@
                 pass_near(k, 0, 1).start()
             if d == 3:
                 pass_near(k, 1, 0).start()
-    for k in range(3):
-        for side in range(2):
+
+    def pass_relayed(side):
+        for k in range(3):
             q = spot_of(k, 3 if side else 1)
             pass_relay(k, side).wait_recv()
 
@@ -232,6 +285,21 @@
                     own[k][q, 16 * side + n] = own[k][q, 16 * side + n] + relay[k][side, n]
 
             pass_near(k, side, side).start()
+
+    turns = (2, 1, 3, 0)
+    give_away(2)
+    give_away(1)
+    take_in(2)
+    give_away(3)
+    take_in(1)
+    give_away(0)
+    p_all.finish()
+    s_all.finish()
+    x_col[own_row, :] = jnp.dot(p_row[...], s_col[...], preferred_element_type=jnp.float32).astype(jnp.bfloat16)
+    take_in(3)
+    pass_relayed(0)
+    pass_relayed(1)
+    take_in(0)
     for k in range(3):
         q = spot_of(k, 0)
         for side in range(2):
@@ -247,6 +315,7 @@
 
         for d in (2, 1, 3):
             pass_on(1, k, d).start()
+    x_all.begin()
 
     def added(stage, k, n):
         mine = sources[stage][k][here[ORDERS[k][stage]], n].astype(jnp.float32)
@@ -262,6 +331,7 @@
                 two[k][q, b] = added(1, k, q * 2 + b)
         for d in (2, 1, 3):
             pass_on(2, k, d).start()
+    x_all.second()
 
     core_row = pl.multiple_of(here["core"] * size, size)
     for k in range(3):
@@ -271,24 +341,24 @@
             cols = pl.ds(pl.multiple_of(tile_column(here) * tile + b * size, size), size)
             row_buf[pl.ds(core_row + STARTS[k], SHARES[k]), cols] = added(2, k, b)
 
-    def tile_of(spot):
-        cols = pl.ds(pl.multiple_of(tile_column(spot) * tile, tile), tile)
+    def tile_of(steps, image):
+        cols = pl.ds(pl.multiple_of(tile_column(p_all.spot(steps, image)) * tile, tile), tile)
         return row_buf.at[pl.ds(core_row, size), cols]
 
-    def spread(dz, dx):
-        at = dz * 2 + dx
-        return remote(tile_of(here), tile_of(here), gather_send.at[at], gather_recv.at[at], in_row(here, dz, dx))
-
-    def share(dz, dx):
-        at = dz * 2 + dx
-        from_there = tile_of(in_row(here, 4 - dz, dx))
-        return remote(from_there, from_there, share_send.at[at], share_recv.at[at], partner)
+    def spread(steps, image):
+        at = steps * 2 + image
+        return remote(tile_of(0, 0), tile_of(0, 0), gather_send.at[at], gather_recv.at[at], p_all.spot(steps, image))
+
+    def share(steps, image):
+        ref = tile_of((4 - steps) % 4, image)
+        at = steps * 2 + image
+        return remote(ref, ref, share_send.at[at], share_recv.at[at], partner)
 
     for step in STEPS:
         spread(*step).start()
     share(0, 0).start()
-    for step in STEPS:
-        send_x(*step).wait_recv()
+    x_all.third()
+    x_all.finish()
     for step in STEPS[::-1]:
         spread(*step).wait_recv()
         share(*step).start()
@@ -296,9 +366,11 @@
         share(*step).wait_recv()
     out_ref[...] = jnp.dot(row_buf[...], x_col[...], preferred_element_type=jnp.float32)
 
+    for gather in (p_all, s_all, x_all):
+        gather.sent()
     for step in STEPS:
-        for copy in (send_p, send_s, send_x, spread, share):
-            copy(*step).wait_send()
+        spread(*step).wait_send()
+        share(*step).wait_send()
     share(0, 0).wait_send()
     for k in range(3):
         for d in turns:
@@ -339,7 +411,7 @@
             plain(2 * size, depth), plain(depth, 2 * size), plain(depth, 2 * size), plain(2 * size, depth),
             dma((atoms,)), dma((3, 4)), dma((3, 4)), dma((3, 2)), dma((3, 2)), dma((3, 2, 2)), dma((3, 2, 2)),
             dma((2, 3, 3)), dma((2, 3, 3)),
-            *[dma((8,)) for _ in range(10)],
+            *[dma((9,)) for _ in range(6)], *[dma((8,)) for _ in range(4)],
         ],
         compiler_params=pltpu.CompilerParams(
             collective_id=0, has_side_effects=True, vmem_limit_bytes=60 << 20

time: 89.5 us -> 75.1 us (0.84)
  Pallas kernels: 81.9 us -> 67.5 us
    pallas_call x1, Pallas kernels: 81.9 us -> 67.5 us  [gradient_tile(): pl.pallas_call(whole_kernel, out_shape=jax.ShapeDtypeStruct((2 * size, 2...]
where the time goes in v3:
time: 75.1 us; the launch traced here: 74.8 us
  Pallas kernels  67.5 us (90%)
  other arithmetic  5.29 us (7%)
  local copies, waits for them, and re-layouts  1.99 us (3%)
    pallas_call x1, Pallas kernels, gradient_tile(): pl.pallas_call(whole_kernel, out_shape=jax.ShapeDtypeStruct((2 * size, 2...  67.5 us
    mul x1, other arithmetic, masked_blocks(): shaped * factor  1.75 us
    unnamed x2, local copies, waits for them, and re-layouts  1.71 us

profile of v3, /device:TPU:1, one launch (start us, length us, event | category | flops | bytes accessed | tf_op | source)
XLA Modules:
  0.0 74.8 jit_solution(5783917748038863643)
XLA Ops:
  0.0 0.7 convert_element_type.7
  0.7 0.1 mul.64
  0.9 0.7 convert_element_type.6
  1.6 0.1 mul.61
  1.7 1.7 %bitcast_multiply_fusion = (bf16[256,256]{1,0:T(8,128)(2,1)}, bf16[256,256]{1,0:T(8,128)(2,1)}) fusion(bf16[256,256]{1,0:T(8,128)(2,1)} %param.14, bf16[32,8,2,128]{3,2,1,0:T(2,128)(2,1)S(1)} %bitcast.16, bf16[256,512]{1,0:T(8,128)(2,1)S(1)} %bitcast.15, s32[]{:T(128)S(6)} %select_n.34, bf16[256,512]{1,0:T(8,128)(2,1)} %param.16), kind=kLoop, calls=%fused_computation.1 | loop fusion | flops 524288 | bytes 786436 | tf_op jit(solution)/shard_map/mul | solution.py:17
  3.5 0.8 %add_bitcast_fusion = s32[128]{0:T(128)S(1)} fusion(s32[2,128]{1,0:T(2,128)} %param.11), kind=kLoop, calls=%fused_computation.17 | loop fusion | flops 512 | bytes 1536 | tf_op jit(solution)/shard_map/jit(_where)/broadcast_in_dim | solution.py:447
  4.2 0.7 bitcast_add_fusion
  4.9 0.1 select_reduce_fusion
  5.0 0.6 compare_select_fusion.4
  5.6 67.5 %shard_map.91 = f32[256,256]{1,0:T(8,128)} custom-call(s32[256]{0:T(256)} %get-tuple-element.8.first_ref, s32[256]{0:T(256)} %get-tuple-element.7.second_ref, f32[16,128]{1,0:T(8,128)} %bitcast.17, bf16[16,2048,128]{2,1,0:T(8,128)(2,1)} %basis_ref.1, bf16[256,256]{1,0:T(8,128)(2,1)} %get-tuple-element.9.density_ref, ...), custom_call_target="tpu_custom_call" | custom-call | flops 17179869184 | bytes 20971520 | tf_op jit(solution)/shard_map/pallas_call | solution.py:400
  73.2 1.7 %copy.16 = f32[256,256]{1,0:T(8,128)} copy(f32[256,256]{1,0:T(8,128)} %shard_map.91) | data formatting | bytes 524288
  (1 shorter events, 0.0 us)

commit v4 on v3

--- a/solution.py
+++ b/solution.py
@@ -8,13 +8,6 @@
 from jax.sharding import PartitionSpec as P
 
 ALL = ("row", "col", "panel")
-
-
-def masked_blocks(matrix, block_mask, block_size):
-    mask_rows, mask_cols = block_mask.shape
-    shaped = matrix.reshape(mask_rows, block_size, mask_cols, block_size)
-    factor = block_mask.astype(matrix.dtype)[:, None, :, None]
-    return (shaped * factor).reshape(mask_rows * block_size, mask_cols * block_size)
 
 
 SIZE = 128
@@ -109,13 +102,14 @@
 
 
 def whole_kernel(
-    first_ref, second_ref, weight_ref, basis_ref, density_ref, inverse_ref, out_ref,
-    raw, left, right, blocks, column,
+    owner_ref, block_ref, atoms_ref, weight_ref, basis_ref,
+    density_ref, density_mask_ref, inverse_ref, inverse_mask_ref, out_ref,
+    table, index_ref, inverse_half, raw, left, right, blocks, column,
     own0, own1, own2, give0, give1, give2, pair0, pair1, pair2,
     relay0, relay1, relay2, near0, near1, near2, one0, one1, one2,
     got20, got21, got22, two0, two1, two2, got30, got31, got32,
     p_row, s_col, x_col, row_buf,
-    fetch_sem, pair_send, pair_recv, relay_send, relay_recv, near_send, near_recv, send_sem, recv_sem,
+    table_sem, half_sem, fetch_sem, pair_send, pair_recv, relay_send, relay_recv, near_send, near_recv, send_sem, recv_sem,
     p_send, p_recv, s_send, s_recv, x_send, x_recv, gather_send, gather_recv, share_send, share_recv,
 ):
     here = place()
@@ -132,6 +126,10 @@
     def fetch(a):
         return pltpu.make_async_copy(basis_ref.at[a], raw.at[a % slots], fetch_sem.at[a])
 
+    tile = 2 * size
+    half_cols = pl.ds(pl.multiple_of(here["core"] * tile, tile), tile)
+    fetch_half = pltpu.make_async_copy(inverse_ref.at[:, half_cols], inverse_half, half_sem)
+    fetch_half.start()
     for a in range(slots):
         fetch(a).start()
 
@@ -146,6 +144,24 @@
     for k in range(chunks):
         spread_row = jnp.broadcast_to(weight_ref[k : k + 1, :], (size, size))
         column[k * size : (k + 1) * size, :] = spread_row.T
+
+    def upright(row):
+        return jnp.broadcast_to(row, (size, size)).T
+
+    count = owner_ref.shape[1]
+    serial = lax.broadcasted_iota(jnp.int32, (1, count), 1)
+    target = upright(owner_ref[...] * 2 + block_ref[...])
+    key = upright((serial * atoms + atoms_ref[0:1, :]) * atoms + atoms_ref[1:2, :])
+    lane = lax.broadcasted_iota(jnp.int32, (size, size), 1)
+    for part in range(table.shape[1] // size):
+        hit = target == lane + part * size
+        low = jnp.min(jnp.where(hit, key, 1 << 30), axis=0, keepdims=True)
+        high = jnp.max(jnp.where(hit, key, -1), axis=0, keepdims=True)
+        cols = pl.ds(part * size, size)
+        table[0:1, cols] = jnp.where(high >= 0, low % (atoms * atoms), atoms * atoms)
+        table[1:2, cols] = jnp.where(high > low, high % (atoms * atoms), atoms * atoms)
+    fetch_table = pltpu.make_async_copy(table, index_ref, table_sem)
+    fetch_table.start()
     blocks[atoms * atoms] = jnp.zeros((size, size), jnp.bfloat16)
 
     def remote(src, dst, send, recv, spot):
@@ -154,7 +170,6 @@
             device_id=device_at(spot), device_id_type=mesh,
         )
 
-    tile = 2 * size
     own_col = pl.ds(pl.multiple_of(tile_column(here) * tile, tile), tile)
     own_row = pl.ds(pl.multiple_of(tile_row(here) * tile, tile), tile)
 
@@ -173,8 +188,17 @@
     s_all = Gather(here, "y", "x_lo", row_view(s_col), s_send, s_recv)
     x_all = Gather(here, "y", "x_lo", row_view(x_col), x_send, x_recv)
 
-    p_row[:, own_col] = density_ref[...]
-    s_col[own_row, :] = inverse_ref[...]
+    def masked(block, keep):
+        return (block.astype(jnp.float32) * keep.astype(jnp.float32)).astype(jnp.bfloat16)
+
+    fetch_half.wait()
+    for i in range(2):
+        for j in range(2):
+            rows, cols = pl.ds(i * size, size), pl.ds(j * size, size)
+            own_rows = pl.ds(pl.multiple_of(tile_row(here) * tile + i * size, size), size)
+            own_cols = pl.ds(pl.multiple_of(tile_column(here) * tile + j * size, size), size)
+            p_row[rows, own_cols] = masked(density_ref[rows, cols], density_mask_ref[i, j])
+            s_col[own_rows, cols] = masked(inverse_half[rows, cols], inverse_mask_ref[i, here["core"] * 2 + j])
     pl.semaphore_wait(barrier, len(peers))
     p_all.begin()
     s_all.begin()
@@ -212,11 +236,14 @@
     def spot_of(k, d):
         return (here[ORDERS[k][0]] + d) % 4
 
-    def assembled(k, q, m, g, core):
+    def assembled(k, q, m, g, core, also=None):
         at = dict(zip(ORDERS[k], (q, m, g // 2)))
         n = ((tile_row(at) * 8 + tile_column(at)) * 2 + core) * 2 + g % 2
         rows = pl.ds(STARTS[k], SHARES[k])
-        return blocks[first_ref[n], rows, :] + blocks[second_ref[n], rows, :]
+        if also is None:
+            return blocks[index_ref[0, n], rows, :] + blocks[index_ref[1, n], rows, :]
+        total = blocks[index_ref[0, n], rows, :].astype(jnp.float32) + blocks[index_ref[1, n], rows, :].astype(jnp.float32)
+        return (total + also.astype(jnp.float32)).astype(jnp.bfloat16)
 
     def swap(k, d):
         q = spot_of(k, d)
@@ -263,7 +290,7 @@
             @pl.loop(0, 4)
             def _(m):
                 for g in range(8):
-                    own[k][q, m * 8 + g] = assembled(k, q, m, g, here["core"]) + pair[k][q, m * 8 + g]
+                    own[k][q, m * 8 + g] = assembled(k, q, m, g, here["core"], pair[k][q, m * 8 + g])
 
             if d == 2:
                 pass_relay(k, 0).start()
@@ -287,6 +314,7 @@
             pass_near(k, side, side).start()
 
     turns = (2, 1, 3, 0)
+    fetch_table.wait()
     give_away(2)
     give_away(1)
     take_in(2)
@@ -384,7 +412,7 @@
                 pass_on(stage, k, d).wait_send()
 
 
-def gradient_tile(first, second, weights, basis, density, inverse):
+def gradient_tile(owner, block, pairs, weights, basis, density, density_mask, inverse, inverse_mask):
     atoms, points, size = basis.shape
     depth = 16 * size
 
@@ -397,19 +425,21 @@
     dma = pltpu.SemaphoreType.DMA
     vmem = pl.BlockSpec(memory_space=pltpu.VMEM)
     smem = pl.BlockSpec(memory_space=pltpu.SMEM)
+    hbm = pl.BlockSpec(memory_space=pl.ANY)
     return pl.pallas_call(
         whole_kernel,
         out_shape=jax.ShapeDtypeStruct((2 * size, 2 * size), jnp.float32),
-        in_specs=[smem, smem, vmem, pl.BlockSpec(memory_space=pl.ANY), vmem, vmem],
+        in_specs=[vmem, vmem, vmem, vmem, hbm, vmem, smem, hbm, smem],
         out_specs=vmem,
         scratch_shapes=[
+            pltpu.VMEM((2, 2 * size), jnp.int32), pltpu.SMEM((2, 2 * size), jnp.int32), plain(2 * size, 2 * size),
             plain(atoms // 2, points, size), plain(atoms * size, points), plain(points, atoms * size),
             plain(atoms * atoms + 1, size, size), pltpu.VMEM((points, size), jnp.float32),
             *buffers(4, 32), *buffers(4, 32), *buffers(4, 32),
             *buffers(2, 16), *buffers(2, 32), *buffers(4, 8),
             *buffers(3, 8), *buffers(4, 2), *buffers(3, 2),
             plain(2 * size, depth), plain(depth, 2 * size), plain(depth, 2 * size), plain(2 * size, depth),
-            dma((atoms,)), dma((3, 4)), dma((3, 4)), dma((3, 2)), dma((3, 2)), dma((3, 2, 2)), dma((3, 2, 2)),
+            dma, dma, dma((atoms,)), dma((3, 4)), dma((3, 4)), dma((3, 2)), dma((3, 2)), dma((3, 2, 2)), dma((3, 2, 2)),
             dma((2, 3, 3)), dma((2, 3, 3)),
             *[dma((9,)) for _ in range(6)], *[dma((8,)) for _ in range(4)],
         ],
@@ -419,7 +449,10 @@
         cost_estimate=pl.CostEstimate(
             flops=2 * (atoms * size) ** 2 * points, bytes_accessed=20 << 20, transcendentals=0
         ),
-    )(first, second, weights.reshape(-1, size), basis, density, inverse)
+    )(
+        owner.reshape(1, -1), block.reshape(1, -1), pairs, weights.reshape(-1, size), basis,
+        density, density_mask, inverse, inverse_mask,
+    )
 
 
 def local(
@@ -433,26 +466,17 @@
     inverse_intersection,
     inverse_mask,
 ):
-    atoms, _, size = basis_values.shape
-    tile_blocks = density_mask.shape[0]
-    devices = lax.axis_size(ALL)
-    per_owner = tile_blocks * tile_blocks // lax.axis_size("panel")
-    empty = atoms * atoms
-
-    target = target_device[:, 0] * per_owner + target_block
-    serial = jnp.arange(target.shape[0], dtype=jnp.int32)
-    key = serial * empty + pair_atoms[0] * atoms + pair_atoms[1]
-    hit = target[None, :] == jnp.arange(devices * per_owner, dtype=jnp.int32)[:, None]
-    low = jnp.min(jnp.where(hit, key[None, :], 1 << 30), axis=1)
-    high = jnp.max(jnp.where(hit, key[None, :], -1), axis=1)
-    first = jnp.where(high >= 0, low % empty, empty)
-    second = jnp.where(high > low, high % empty, empty)
-
-    density_used = masked_blocks(density, density_mask, size)
-    inverse_used = masked_blocks(inverse_intersection, inverse_mask, size)
-    width = inverse_used.shape[1] // lax.axis_size("panel")
-    own = lax.dynamic_slice_in_dim(inverse_used, lax.axis_index("panel") * width, width, 1)
-    return gradient_tile(first, second, potential, basis_values, density_used, own)
+    return gradient_tile(
+        target_device,
+        target_block,
+        pair_atoms,
+        potential,
+        basis_values,
+        density,
+        density_mask,
+        inverse_intersection,
+        inverse_mask,
+    )
 
 
 def solution(mesh):

time: 75.1 us -> 69.9 us (0.931)
  other arithmetic: 5.29 us -> 0 us
    mul x1 -> x0, other arithmetic: 1.75 us -> none  [masked_blocks(): shaped * factor]
    convert_element_type x2 -> x0, other arithmetic: 1.37 us -> none  [masked_blocks(): factor = block_mask.astype(matrix.dtype)[:, None, :, None]]
    broadcast_in_dim x1 -> x0, other arithmetic: 0.76 us -> none  [local(): high = jnp.max(jnp.where(hit, key[None, :], -1), axis=1)]
    unnamed x2 -> x1, local copies, waits for them, and re-layouts: 1.71 us -> 1.67 us
where the time goes in v4:
time: 69.9 us; the launch traced here: 69.7 us
  Pallas kernels  68 us (97%)
  local copies, waits for them, and re-layouts  1.67 us (2%)
    pallas_call x1, Pallas kernels, gradient_tile(): pl.pallas_call(whole_kernel, out_shape=jax.ShapeDtypeStruct((2 * size, 2...  68 us
    unnamed x1, local copies, waits for them, and re-layouts  1.67 us

profile of v4, /device:TPU:1, one launch (start us, length us, event | category | flops | bytes accessed | tf_op | source)
XLA Modules:
  0.0 69.7 jit_solution(17847854350469405181)
XLA Ops:
  0.0 68.0 %shard_map.91 = f32[256,256]{1,0:T(8,128)} custom-call(s32[1,128]{1,0:T(1,128)} %bitcast.4, s32[1,128]{1,0:T(1,128)} %bitcast.5, s32[2,128]{1,0:T(2,128)} %atoms_ref.1, f32[16,128]{1,0:T(8,128)} %bitcast.3, bf16[16,2048,128]{2,1,0:T(8,128)(2,1)} %basis_ref.1, bf16[256,256]{1,0:T(8,128)(2,1)} %density_ref.1, s32[2,2]{1,0:T(2,128)} %density_mask_ref.1, ...), custom_call_target="tpu_custom_call" | custom-call | flops 17179869184 | bytes 20971520 | tf_op jit(solution)/shard_map/pallas_call | solution.py:429
  68.0 1.7 %copy.11 = f32[256,256]{1,0:T(8,128)} copy(f32[256,256]{1,0:T(8,128)} %shard_map.91) | data formatting | bytes 524288

commit v5 on v4

--- a/solution.py
+++ b/solution.py
@@ -102,8 +102,8 @@
 
 
 def whole_kernel(
-    owner_ref, block_ref, atoms_ref, weight_ref, basis_ref,
-    density_ref, density_mask_ref, inverse_ref, inverse_mask_ref, out_ref,
+    owner_in, block_in, atoms_in, weight_in, basis_ref, density_in, density_mask_in, inverse_ref, inverse_mask_in, out_ref,
+    owner_ref, block_ref, atoms_ref, weight_ref, density_ref, density_mask_ref, inverse_mask_ref, small_sem,
     table, index_ref, inverse_half, raw, left, right, blocks, column,
     own0, own1, own2, give0, give1, give2, pair0, pair1, pair2,
     relay0, relay1, relay2, near0, near1, near2, one0, one1, one2,
@@ -126,13 +126,6 @@
     def fetch(a):
         return pltpu.make_async_copy(basis_ref.at[a], raw.at[a % slots], fetch_sem.at[a])
 
-    tile = 2 * size
-    half_cols = pl.ds(pl.multiple_of(here["core"] * tile, tile), tile)
-    fetch_half = pltpu.make_async_copy(inverse_ref.at[:, half_cols], inverse_half, half_sem)
-    fetch_half.start()
-    for a in range(slots):
-        fetch(a).start()
-
     peers = [partner]
     for axis in ("x", "y", "z"):
         peers += [moved(here, axis, d) for d in (1, 2, 3)]
@@ -141,6 +134,26 @@
     for peer in peers:
         pl.semaphore_signal(barrier, inc=1, device_id=device_at(peer), device_id_type=mesh)
 
+    tile = 2 * size
+    half_cols = pl.ds(pl.multiple_of(here["core"] * tile, tile), tile)
+    fetch_half = pltpu.make_async_copy(inverse_ref.at[:, half_cols], inverse_half, half_sem)
+    fetch_half.start()
+    small = [
+        pltpu.make_async_copy(source, held, small_sem.at[i])
+        for i, (source, held) in enumerate(
+            (
+                (weight_in, weight_ref), (owner_in, owner_ref), (block_in, block_ref), (atoms_in, atoms_ref),
+                (density_in, density_ref), (density_mask_in, density_mask_ref), (inverse_mask_in, inverse_mask_ref),
+            )
+        )
+    ]
+    for copy in small:
+        copy.start()
+    for a in range(slots):
+        fetch(a).start()
+
+    for copy in small:
+        copy.wait()
     for k in range(chunks):
         spread_row = jnp.broadcast_to(weight_ref[k : k + 1, :], (size, size))
         column[k * size : (k + 1) * size, :] = spread_row.T
@@ -328,22 +341,21 @@
     pass_relayed(0)
     pass_relayed(1)
     take_in(0)
+    x_all.begin()
     for k in range(3):
         q = spot_of(k, 0)
         for side in range(2):
             for part in range(2):
                 pass_near(k, side, part).wait_recv()
 
-        @pl.loop(0, 4)
-        def _(m):
+        for d in turns:
+            m = (here[ORDERS[k][1]] + d) % 4
             for g in range(8):
                 n = m * 8 + g
                 total = own[k][q, n].astype(jnp.float32) + near[k][0, n].astype(jnp.float32)
                 one[k][m, g] = (total + near[k][1, n].astype(jnp.float32)).astype(jnp.bfloat16)
-
-        for d in (2, 1, 3):
-            pass_on(1, k, d).start()
-    x_all.begin()
+            if d:
+                pass_on(1, k, d).start()
 
     def added(stage, k, n):
         mine = sources[stage][k][here[ORDERS[k][stage]], n].astype(jnp.float32)
@@ -354,11 +366,12 @@
     for k in range(3):
         for d in (1, 2, 3):
             pass_on(1, k, d).wait_recv()
-        for q in range(4):
+        for d in turns:
+            q = (here[ORDERS[k][2]] + d) % 4
             for b in range(2):
                 two[k][q, b] = added(1, k, q * 2 + b)
-        for d in (2, 1, 3):
-            pass_on(2, k, d).start()
+            if d:
+                pass_on(2, k, d).start()
     x_all.second()
 
     core_row = pl.multiple_of(here["core"] * size, size)
@@ -390,9 +403,14 @@
     for step in STEPS[::-1]:
         spread(*step).wait_recv()
         share(*step).start()
+    def finish_rows(start):
+        rows = pl.ds(pl.multiple_of(start, size), size)
+        out_ref[rows, :] = jnp.dot(row_buf[rows, :], x_col[...], preferred_element_type=jnp.float32)
+
+    finish_rows(core_row)
     for step in ((0, 0),) + STEPS:
         share(*step).wait_recv()
-    out_ref[...] = jnp.dot(row_buf[...], x_col[...], preferred_element_type=jnp.float32)
+    finish_rows(size - core_row)
 
     for gather in (p_all, s_all, x_all):
         gather.sent()
@@ -424,14 +442,17 @@
 
     dma = pltpu.SemaphoreType.DMA
     vmem = pl.BlockSpec(memory_space=pltpu.VMEM)
-    smem = pl.BlockSpec(memory_space=pltpu.SMEM)
     hbm = pl.BlockSpec(memory_space=pl.ANY)
     return pl.pallas_call(
         whole_kernel,
         out_shape=jax.ShapeDtypeStruct((2 * size, 2 * size), jnp.float32),
-        in_specs=[vmem, vmem, vmem, vmem, hbm, vmem, smem, hbm, smem],
+        in_specs=[hbm] * 9,
         out_specs=vmem,
         scratch_shapes=[
+            pltpu.VMEM((1, owner.shape[0]), jnp.int32), pltpu.VMEM((1, owner.shape[0]), jnp.int32),
+            pltpu.VMEM(pairs.shape, jnp.int32), pltpu.VMEM((points // size, size), jnp.float32),
+            plain(*density.shape), pltpu.SMEM(density_mask.shape, jnp.int32), pltpu.SMEM(inverse_mask.shape, jnp.int32),
+            dma((7,)),
             pltpu.VMEM((2, 2 * size), jnp.int32), pltpu.SMEM((2, 2 * size), jnp.int32), plain(2 * size, 2 * size),
             plain(atoms // 2, points, size), plain(atoms * size, points), plain(points, atoms * size),
             plain(atoms * atoms + 1, size, size), pltpu.VMEM((points, size), jnp.float32),

time: 69.9 us -> 67.5 us (0.966)
  Pallas kernels: 68 us -> 65.6 us
    pallas_call x1, Pallas kernels: 68 us -> 65.6 us  [gradient_tile(): pl.pallas_call(whole_kernel, out_shape=jax.ShapeDtypeStruct((2 * size, 2...]
where the time goes in v5:
time: 67.5 us; the launch traced here: 67.3 us
  Pallas kernels  65.6 us (97%)
  local copies, waits for them, and re-layouts  1.67 us (2%)
    pallas_call x1, Pallas kernels, gradient_tile(): pl.pallas_call(whole_kernel, out_shape=jax.ShapeDtypeStruct((2 * size, 2...  65.6 us
    unnamed x1, local copies, waits for them, and re-layouts  1.67 us

profile of v5, /device:TPU:1, one launch (start us, length us, event | category | flops | bytes accessed | tf_op | source)
XLA Modules:
  0.0 67.3 jit_solution(7598752134931070246)
XLA Ops:
  0.0 65.6 %shard_map.91 = f32[256,256]{1,0:T(8,128)} custom-call(s32[1,128]{1,0:T(1,128)} %bitcast.4, s32[1,128]{1,0:T(1,128)} %bitcast.5, s32[2,128]{1,0:T(2,128)} %atoms_in.1, f32[16,128]{1,0:T(8,128)} %bitcast.3, bf16[16,2048,128]{2,1,0:T(8,128)(2,1)} %basis_ref.1, bf16[256,256]{1,0:T(8,128)(2,1)} %density_in.1, s32[2,2]{1,0:T(2,128)} %density_mask_in.1, ...), custom_call_target="tpu_custom_call" | custom-call | flops 17179869184 | bytes 20971520 | tf_op jit(solution)/shard_map/pallas_call | solution.py:446
  65.6 1.7 %copy.11 = f32[256,256]{1,0:T(8,128)} copy(f32[256,256]{1,0:T(8,128)} %shard_map.91) | data formatting | bytes 524288

commit v6 on v5

--- a/solution.py
+++ b/solution.py
@@ -72,6 +72,9 @@
 
     def begin(self):
         self.cross().start()
+        self.begin_ring()
+
+    def begin_ring(self):
         self.hop(0, 0).start()
         self.hop(1, 0).start()
 
@@ -338,10 +341,10 @@
     s_all.finish()
     x_col[own_row, :] = jnp.dot(p_row[...], s_col[...], preferred_element_type=jnp.float32).astype(jnp.bfloat16)
     take_in(3)
+    x_all.begin_ring()
     pass_relayed(0)
     pass_relayed(1)
     take_in(0)
-    x_all.begin()
     for k in range(3):
         q = spot_of(k, 0)
         for side in range(2):
@@ -356,6 +359,8 @@
                 one[k][m, g] = (total + near[k][1, n].astype(jnp.float32)).astype(jnp.bfloat16)
             if d:
                 pass_on(1, k, d).start()
+
+    x_all.cross().start()
 
     def added(stage, k, n):
         mine = sources[stage][k][here[ORDERS[k][stage]], n].astype(jnp.float32)

time: 67.5 us -> 67.6 us (level)
  no operation moved by 1% of the time
where the time goes in v6:
time: 67.6 us; the launch traced here: 67.5 us
  Pallas kernels  65.8 us (97%)
  local copies, waits for them, and re-layouts  1.67 us (2%)
    pallas_call x1, Pallas kernels, gradient_tile(): pl.pallas_call(whole_kernel, out_shape=jax.ShapeDtypeStruct((2 * size, 2...  65.8 us
    unnamed x1, local copies, waits for them, and re-layouts  1.67 us

profile of v6, /device:TPU:1, one launch (start us, length us, event | category | flops | bytes accessed | tf_op | source)
XLA Modules:
  0.0 67.5 jit_solution(9868186222508586349)
XLA Ops:
  0.0 65.8 %shard_map.91 = f32[256,256]{1,0:T(8,128)} custom-call(s32[1,128]{1,0:T(1,128)} %bitcast.4, s32[1,128]{1,0:T(1,128)} %bitcast.5, s32[2,128]{1,0:T(2,128)} %atoms_in.1, f32[16,128]{1,0:T(8,128)} %bitcast.3, bf16[16,2048,128]{2,1,0:T(8,128)(2,1)} %basis_ref.1, bf16[256,256]{1,0:T(8,128)(2,1)} %density_in.1, s32[2,2]{1,0:T(2,128)} %density_mask_in.1, ...), custom_call_target="tpu_custom_call" | custom-call | flops 17179869184 | bytes 20971520 | tf_op jit(solution)/shard_map/pallas_call | solution.py:451
  65.8 1.7 %copy.11 = f32[256,256]{1,0:T(8,128)} copy(f32[256,256]{1,0:T(8,128)} %shard_map.91) | data formatting | bytes 524288
